TPU v7x, 32 devices: a whole 2x2x4 slice. The times are simulated.
32 devices in a mesh: energy: 16 (over z, y, core), space: 2 (over x).
Axes of the slice: x: 2, y: 2, z: 4, core: 2. Of those that a mesh axis runs over, the one named last changes fastest.
Arguments:
- distribution: bfloat16 [96, 9, 8, 3072], P('energy', None, 'space'), may hold values from -6 to 6
- region_map: int32 [8, 3072], P('space'), may hold values from 0 to 3
- contact_mask: int32 [8, 3072], P('space'), may hold values 0 or 1
- doping_levels: float32 [4], replicated, may hold values from -2 to 2
- coupling: bfloat16 [2, 3, 9, 9], replicated, may hold values from -1.796875 to 1.796875
- level_coef: float32 [96, 3], P('energy'), may hold values from 0.3 to 1.2
- phonon_kernel: float32 [2, 96, 9], P(None, 'energy'), may hold values from 0.2 to 1
- out_rate: float32 [96, 9], P('energy'), may hold values from 0.5 to 2
Outputs:
- updated: bfloat16 [96, 9, 8, 3072], P('energy', None, 'space')
- potential: float32 [8, 3072], P('space')
All inputs are finite; a program needn't handle non-finite values. No bound on the sum of `contact_mask` on one device may be relied on, other than what follows from the above.
Results may differ from a plain program's by a relative error of at most 0.0006.
Values may be sent and summed in bfloat16 or wider, within the bound.
A program may use at most 128 MiB of HBM per device.

v0:
```python
import math

import jax
import jax.numpy as jnp
from jax import lax
from jax.sharding import PartitionSpec as P

Y = 64
Z = 48
SHIFT = 6
REGIONS = 4


step_time = 0.4
contact_rate = 2.0
highest = lax.Precision.HIGHEST


def extended(cells, sides, width):
    for axis, dim in sides:
        count = lax.axis_size(axis)
        ends = count - 1
        head = lax.slice_in_dim(cells, 0, width, axis=dim)
        tail = lax.slice_in_dim(cells, cells.shape[dim] - width, cells.shape[dim], axis=dim)
        cells = jnp.concatenate(
            [
                lax.ppermute(tail, axis, [(i, (i + 1) % count) for i in range(ends)]),
                cells,
                lax.ppermute(head, axis, [((i + 1) % count, i) for i in range(ends)]),
            ],
            axis=dim,
        )
    return cells


def sine_table(count):
    indices = jnp.arange(count, dtype=jnp.float32) + 1.0
    angles = math.pi * indices[:, None] * indices[None, :] / (count + 1)
    return math.sqrt(2.0 / (count + 1)) * jnp.sin(angles)


def eigen_row(count):
    indices = jnp.arange(count, dtype=jnp.float32) + 1.0
    return 2.0 - 2.0 * jnp.cos(math.pi * indices / (count + 1))


def difference_table(count):
    rows_index = jnp.arange(count, dtype=jnp.int32)[:, None]
    cols_index = jnp.arange(count, dtype=jnp.int32)[None, :]
    return 0.5 * (cols_index == rows_index - 1).astype(jnp.float32) - 0.5 * (
        cols_index == rows_index + 1
    ).astype(jnp.float32)


def back_minus_front(values, dimension):
    length = values.shape[dimension]
    widths = [(0, 0)] * values.ndim
    widths[dimension] = (1, 1)
    padded = jnp.pad(values, widths)
    return 0.5 * (
        lax.slice_in_dim(padded, 0, length, axis=dimension)
        - lax.slice_in_dim(padded, 2, length + 2, axis=dimension)
    )


def yz_transform(values, table_y, table_z):
    shape_front = values.shape[:-1]
    cube_values = values.reshape(shape_front + (Y, Z))
    turned = jnp.einsum("...bc,bj,ck->...jk", cube_values, table_y, table_z, precision=highest)
    return turned.reshape(shape_front + (Y * Z,))


def harmonic_mix(matrix, values):
    return jnp.einsum("hk,ekxc->ehxc", matrix, values, preferred_element_type=jnp.float32)


def solve_pencil(charge_modes, mode_base, eigen_yz):
    rows_local, mode_count = charge_modes.shape
    slab_count = lax.axis_size("space")
    piece = mode_count // slab_count
    blocks = charge_modes.reshape(rows_local, slab_count, piece)
    pencil = lax.all_to_all(blocks, "space", split_axis=1, concat_axis=0, tiled=True)
    total_rows = rows_local * slab_count
    pencil = pencil.reshape(total_rows, piece)
    start = mode_base + lax.axis_index("space") * piece
    eigen_part = lax.dynamic_slice_in_dim(eigen_yz, start, piece, 0)
    table_x = sine_table(total_rows)
    spectral = jnp.dot(table_x, pencil, precision=highest)
    spectral = spectral / (eigen_row(total_rows)[:, None] + eigen_part[None, :])
    potential_x = jnp.dot(table_x, spectral, precision=highest)
    field_x = jnp.dot(difference_table(total_rows), potential_x, precision=highest)
    stacked = jnp.stack([potential_x, field_x]).reshape(2, total_rows, 1, piece)
    returned = lax.all_to_all(stacked, "space", split_axis=1, concat_axis=2, tiled=True)
    return returned.reshape(2, rows_local, mode_count)


def local(
    distribution,
    region_map,
    contact_mask,
    doping_levels,
    coupling,
    level_coef,
    phonon_kernel,
    out_rate,
):
    local_levels = distribution.shape[0]
    rows_local = distribution.shape[2]
    cell_count = distribution.shape[3]
    total_levels = local_levels * lax.axis_size("energy")
    beside_levels = extended(distribution, (("energy", 0),), SHIFT)
    beside_rows = extended(distribution, (("space", 2),), 1)
    isotropic = distribution[:, 0].astype(jnp.float32)
    partial_value = jnp.einsum(
        "e,exc->xc", level_coef[:, 2], isotropic, precision=highest
    ) / math.sqrt(total_levels)
    doping = jnp.zeros(region_map.shape, jnp.float32)
    for region in range(REGIONS):
        doping = doping + jnp.where(region_map == region, doping_levels[region], 0.0)
    table_y = sine_table(Y)
    table_z = sine_table(Z)
    partial_modes = yz_transform(partial_value, table_y, table_z)
    doping_modes = yz_transform(doping, table_y, table_z)
    eigen_yz = (eigen_row(Y)[:, None] + eigen_row(Z)[None, :]).reshape(Y * Z)
    summed = lax.psum(partial_modes, "energy")
    solved = solve_pencil(summed - doping_modes, 0, eigen_yz)
    solved = yz_transform(solved, table_y, table_z)
    potential = solved[0]
    cube_potential = potential.reshape(rows_local, Y, Z)
    fields = (
        solved[1],
        back_minus_front(cube_potential, 1).reshape(rows_local, cell_count),
        back_minus_front(cube_potential, 2).reshape(rows_local, cell_count),
    )
    depth = jnp.arange(cell_count, dtype=jnp.int32) % Z
    velocity = level_coef[:, 0][:, None, None, None]
    field_pull = 3.0 * level_coef[:, 1][:, None, None, None]
    from_above = beside_levels[2 * SHIFT : 2 * SHIFT + local_levels]
    from_below = beside_levels[:local_levels]
    change = phonon_kernel[0][:, :, None, None] * from_above.astype(jnp.float32) + phonon_kernel[1][
        :, :, None, None
    ] * from_below.astype(jnp.float32)
    mixed_x = harmonic_mix(coupling[0, 0], beside_rows)
    change = change - velocity * (0.5 * (mixed_x[:, :, 2:] - mixed_x[:, :, :-2]))
    mixed_y = harmonic_mix(coupling[0, 1], distribution)
    padded_y = jnp.pad(mixed_y, ((0, 0), (0, 0), (0, 0), (Z, Z)))
    change = change - velocity * (0.5 * (padded_y[..., 2 * Z :] - padded_y[..., :cell_count]))
    mixed_z = harmonic_mix(coupling[0, 2], distribution)
    padded_z = jnp.pad(mixed_z, ((0, 0), (0, 0), (0, 0), (1, 1)))
    change = change - velocity * (
        0.5
        * (
            jnp.where(depth < Z - 1, padded_z[..., 2:], 0.0)
            - jnp.where(depth > 0, padded_z[..., :cell_count], 0.0)
        )
    )
    for direction in range(3):
        change = change + field_pull * fields[direction][None, None] * harmonic_mix(
            coupling[1, direction], distribution
        )
    decay_rate = (
        out_rate[:, :, None, None] + contact_rate * contact_mask.astype(jnp.float32)[None, None]
    )
    updated = (
        (distribution.astype(jnp.float32) + step_time * change) / (1.0 + step_time * decay_rate)
    ).astype(jnp.bfloat16)
    return (updated, potential)


def solution(mesh):
    return jax.shard_map(
        local,
        mesh=mesh,
        in_specs=(
            P("energy", None, "space", None),
            P("space", None),
            P("space", None),
            P(),
            P(),
            P("energy", None),
            P(None, "energy", None),
            P("energy", None),
        ),
        out_specs=(P("energy", None, "space", None), P("space", None)),
        check_vma=False,
    )
```

profile of v0, /device:TPU:0, one launch (start us, length us, event | category | flops | bytes accessed | tf_op | source)
XLA Modules:
  0.0 160.4 jit_solution(16984916188647941049)
XLA Ops:
  0.7 3.6 %collective-permute-start.1 = (bf16[6,9,4,3072]{3,2,1,0:T(4,128)(2,1)}, bf16[6,9,4,3072]{3,2,1,0:T(4,128)(2,1)}, u32[]{:S(2)}, u32[]{:S(2)}) collective-permute-start(bf16[6,9,4,3072]{3,2,1,0:T(4,128)(2,1)} %param.8), channel_id=1, source_target_pairs={{0,2},{2,4},{4,6},{6,8},{8,10},{10,12},{12,14},{14,16},{16,18},{18... | collective-permute-start | bytes 3981320 | tf_op jit(solution)/shard_map/ppermute | solution.py:27
  4.3 1.3 collective-permute-start
  5.6 1.0 slice_bitcast_fusion
  6.6 1.5 fusion.113
  8.1 3.4 %select_add_fusion = f32[4,3072]{1,0:T(4,128)S(1)} fusion(s32[4,3072]{1,0:T(4,128)} %param.9, f32[]{:T(128)} %bitcast.30, f32[]{:T(128)} %bitcast.29, f32[]{:T(128)} %bitcast.28, f32[]{:T(128)} %bitcast.27), kind=kLoop, calls=%fused_computation.58 | loop fusion | flops 135168 | bytes 98320 | tf_op jit(solution)/shard_map/add | solution.py:119
  11.6 0.4 fusion.38
  12.0 0.4 convolution_bitcast_fusion.5
  12.5 0.1 reshape.133
  12.7 1.0 fusion.32
  13.9 0.4 fusion.39
  14.3 0.4 convolution_bitcast_fusion.6
  14.9 72.0 %psum.7 = f32[4,3072]{1,0:T(4,128)S(1)} all-reduce(f32[4,3072]{1,0:T(4,128)S(1)} %reshape.131), channel_id=1, replica_groups=mesh['energy'=16,'space'=2] {'energy'}, use_global_device_ids=true, to_apply=%region_0.1 | all-reduce | flops 12288 | bytes 98304 | tf_op jit(solution)/shard_map/psum | solution.py:125
  86.9 0.6 sub.60
  87.6 3.3 %all-to-all-start = ((f32[4,2,1536]{2,0,1:T(4,128)}), f32[4,2,1536]{2,0,1:T(4,128)S(1)}, u32[]{:S(2)}, u32[]{:S(2)}) async-start(f32[4,2,1536]{2,0,1:T(4,128)} %bitcast.35), calls=%async_computation | async-start | bytes 98304 | tf_op jit(solution)/shard_map/all_to_all | solution.py:82
  90.9 3.0 %fusion.109 = (bf16[6,9,1,3072]{3,2,1,0:T(2,128)(2,1)S(1)}, bf16[6,9,1,3072]{3,2,1,0:T(2,128)(2,1)S(1)}) fusion(bf16[6,9,4,3072]{3,2,1,0:T(4,128)(2,1)} %param.8), kind=kLoop, calls=%fused_computation.162 | loop fusion | bytes 1327104 | tf_op jit(solution)/shard_map/slice | solution.py:24
  93.8 0.1 copy.106
  94.0 1.3 collective-permute-start.3
  95.3 0.1 copy.105
  95.5 4.6 %collective-permute-start.2 = (bf16[6,9,1,3072]{3,0,2,1:T(8,128)(2,1)S(1)}, bf16[6,9,1,3072]{3,0,2,1:T(8,128)(2,1)S(1)}, u32[]{:S(2)}, u32[]{:S(2)}) collective-permute-start(bf16[6,9,1,3072]{3,0,2,1:T(8,128)(2,1)S(1)} %copy.105), channel_id=1, source_target_pairs={{0,1},{2,3},{4,5},{6,7},{8,9},{10,11},{12,13},{14,15},{16,17},{18,... | collective-permute-start | bytes 995336 | tf_op jit(solution)/shard_map/ppermute | solution.py:27
  100.2 0.6 multiply_bitcast_fusion.1
  100.9 0.6 fusion.111
  101.5 0.6 convert_multiply_fusion
  102.1 2.9 %fusion.24 = f32[6,4,3072,9]{2,3,1,0:T(8,128)} fusion(bf16[6,9,4,3072]{3,2,1,0:T(4,128)(2,1)S(1)} %copy-done, bf16[1,1,9,9]{3,0,2,1:T(2,128)(2,1)S(1)} %get-tuple-element.16), kind=kOutput, calls=%fused_computation.34 | convolution fusion | flops 11943936 | bytes 3981474 | tf_op jit(solution)/shard_map/hk,ekxc->ehxc/dot_general | solution.py:74
  105.1 3.0 %convolution_bitcast_fusion.1 = f32[6,9,4,3072]{3,1,2,0:T(8,128)} fusion(bf16[6,9,4,3072]{3,2,1,0:T(4,128)(2,1)S(1)} %copy-done, bf16[1,1,9,9]{3,0,2,1:T(2,128)(2,1)S(1)} %get-tuple-element.17), kind=kOutput, calls=%fused_computation.23 | convolution fusion | flops 11943936 | bytes 3981474 | tf_op jit(solution)/shard_map/hk,ekxc->ehxc/dot_general | solution.py:74
  108.0 3.0 %convolution_bitcast_fusion.2 = f32[6,9,4,3072]{3,1,2,0:T(8,128)} fusion(bf16[6,9,4,3072]{3,2,1,0:T(4,128)(2,1)S(1)} %copy-done, bf16[1,1,9,9]{3,0,2,1:T(2,128)(2,1)S(1)} %get-tuple-element.18), kind=kOutput, calls=%fused_computation.24 | convolution fusion | flops 11943936 | bytes 3981474 | tf_op jit(solution)/shard_map/hk,ekxc->ehxc/dot_general | solution.py:74
  111.1 3.0 %fusion.22 = f32[6,4,3072,9]{2,3,1,0:T(8,128)} fusion(bf16[6,9,4,3072]{3,2,1,0:T(4,128)(2,1)S(1)} %copy-done, bf16[1,1,9,9]{3,0,2,1:T(2,128)(2,1)S(1)} %get-tuple-element.20), kind=kOutput, calls=%fused_computation.32 | convolution fusion | flops 11943936 | bytes 3981474 | tf_op jit(solution)/shard_map/hk,ekxc->ehxc/dot_general | solution.py:74
  114.0 0.6 copy_bitcast_fusion.13
  114.9 0.3 convolution_divide_fusion
  115.2 0.3 fusion.75
  115.5 0.2 convolution_bitcast_fusion.3
  115.8 0.7 copy.78
  116.5 3.5 %all-to-all-start.1 = ((f32[2,8,1,1536]{3,0,2,1:T(2,128)}), f32[2,8,1,1536]{3,0,2,1:T(2,128)S(1)}, u32[]{:S(2)}, u32[]{:S(2)}) async-start(f32[2,8,1,1536]{3,0,2,1:T(2,128)} %copy.78), calls=%async_computation.1 | async-start | bytes 196608 | tf_op jit(solution)/shard_map/all_to_all | solution.py:93
  120.0 0.6 fusion.69
  120.6 2.0 %copy.58 = bf16[6,9,4,3072]{3,1,2,0:T(8,128)(2,1)} copy(bf16[6,9,4,3072]{3,2,1,0:T(4,128)(2,1)S(1)} %copy-done) | data formatting | bytes 2654208 | tf_op args[0]
  122.6 1.5 all-to-all-done.1
  124.2 0.2 reshape_reshape.3
  124.4 0.6 fusion.36
  125.0 0.5 convolution_bitcast_fusion.4
  125.5 0.7 fusion.110
  126.2 0.8 mul.385
  127.0 1.2 subtract_multiply_fusion
  128.7 1.8 %broadcast_multiply_fusion.2 = (f32[6,4,3072]{2,1,0:T(4,128)}, f32[6,4,3072]{2,1,0:T(4,128)}, f32[6,4,3072]{2,1,0:T(4,128)}) fusion(f32[4,3072]{1,0:T(4,128)} %mul.385, f32[6]{0:T(128)} %get-tuple-element.24, f32[4,3072]{1,0:T(4,128)S(1)} %mul.392, f32[4,3072]{1,0:T(4,128)S(1)} %mul.399), kind=kLoop, calls=%fused_computation.47 | loop fusion | flops 221184 | bytes 1032216 | tf_op jit(solution)/shard_map/mul | solution.py:158
  130.6 0.8 squeeze.51
  131.3 0.2 copy.67
  131.5 0.2 copy.65
  131.9 5.9 %convolution_bitcast_fusion = f32[6,9,6,3072]{3,1,2,0:T(8,128)} fusion(bf16[6,9,1,3072]{3,1,2,0:T(8,128)(2,1)S(1)} %copy.67, bf16[6,9,4,3072]{3,1,2,0:T(8,128)(2,1)} %copy.58, bf16[6,9,1,3072]{3,1,2,0:T(8,128)(2,1)S(1)} %copy.65, bf16[1,1,9,9]{3,0,2,1:T(2,128)(2,1)} %get-tuple-element.19), kind=kOutput, calls=%fused_computation | convolution fusion | flops 19906560 | bytes 5972130 | tf_op jit(solution)/shard_map/hk,ekxc->ehxc/dot_general | solution.py:74
  137.9 18.7 %fusion.16 = bf16[6,9,4,3072]{3,1,2,0:T(8,128)(2,1)} fusion(f32[6,4,3072,9]{2,3,1,0:T(8,128)} %fusion.22, f32[6,4,3072,9]{2,3,1,0:T(8,128)} %fusion.24, f32[6,9,4,3072]{3,1,2,0:T(8,128)} %convolution_bitcast_fusion.1, f32[6,9,4,3072]{3,1,2,0:T(8,128)} %convolution_bitcast_fusion.2, f32[6,9,6,3072]{3,1,2,0:T(8,128)} %convolution_bitcast_fusion, ...), kind=kOutput, calls=%fused_computation.22 | convolution fusion | flops 31850496 | bytes 23518208 | tf_op jit(solution)/shard_map/hk,ekxc->ehxc/dot_general | solution.py:74
  156.6 3.8 %copy.91 = bf16[6,9,4,3072]{3,2,1,0:T(4,128)(2,1)} copy(bf16[6,9,4,3072]{3,1,2,0:T(8,128)(2,1)} %fusion.16) | data formatting | bytes 2654208
  (65 shorter events, 1.9 us)
Async XLA Ops:
  0.6 101.5 %copy-start = (bf16[6,9,4,3072]{3,2,1,0:T(4,128)(2,1)S(1)}, bf16[6,9,4,3072]{3,2,1,0:T(4,128)(2,1)}, u32[]{:S(2)}) copy-start(bf16[6,9,4,3072]{3,2,1,0:T(4,128)(2,1)} %param.8) | copy-start | bytes 3981316
  0.6 99.5 %copy-start.8 = (f32[6,3]{0,1:T(4,128)S(1)}, f32[6,3]{0,1:T(4,128)}, u32[]{:S(2)}) copy-start(f32[6,3]{0,1:T(4,128)} %param.13) | copy-start | bytes 220
  0.7 100.2 %copy-start.7 = (f32[2,6,9]{2,0,1:T(2,128)S(1)}, f32[2,6,9]{2,0,1:T(2,128)}, u32[]{:S(2)}) copy-start(f32[2,6,9]{2,0,1:T(2,128)} %param.14) | copy-start | bytes 1300
  0.7 100.2 %copy-start.4 = (bf16[2,3,9,9]{3,0,2,1:T(2,128)(2,1)S(1)}, bf16[2,3,9,9]{3,0,2,1:T(2,128)(2,1)}, u32[]{:S(2)}) copy-start(bf16[2,3,9,9]{3,0,2,1:T(2,128)(2,1)} %param.12) | copy-start | bytes 2920
  0.7 100.8 %copy-start.5 = (s32[4,3072]{1,0:T(4,128)S(1)}, s32[4,3072]{1,0:T(4,128)}, u32[]{:S(2)}) copy-start(s32[4,3072]{1,0:T(4,128)} %param.10) | copy-start | bytes 147460
  0.7 137.1 %collective-permute-start.1 = (bf16[6,9,4,3072]{3,2,1,0:T(4,128)(2,1)}, bf16[6,9,4,3072]{3,2,1,0:T(4,128)(2,1)}, u32[]{:S(2)}, u32[]{:S(2)}) collective-permute-start(bf16[6,9,4,3072]{3,2,1,0:T(4,128)(2,1)} %param.8), channel_id=1, source_target_pairs={{0,2},{2,4},{4,6},{6,8},{8,10},{10,12},{12,14},{14,16},{16,18},{18... | collective-permute-start | bytes 3981320 | tf_op jit(solution)/shard_map/ppermute | solution.py:27
  4.3 133.5 %collective-permute-start = (bf16[6,9,4,3072]{3,2,1,0:T(4,128)(2,1)}, bf16[6,9,4,3072]{3,2,1,0:T(4,128)(2,1)}, u32[]{:S(2)}, u32[]{:S(2)}) collective-permute-start(bf16[6,9,4,3072]{3,2,1,0:T(4,128)(2,1)} %param.8), channel_id=1, source_target_pairs={{2,0},{4,2},{6,4},{8,6},{10,8},{12,10},{14,12},{16,14},{18,16},{20... | collective-permute-start | bytes 3981320 | tf_op jit(solution)/shard_map/ppermute | solution.py:29
  87.6 27.3 %all-to-all-start = ((f32[4,2,1536]{2,0,1:T(4,128)}), f32[4,2,1536]{2,0,1:T(4,128)S(1)}, u32[]{:S(2)}, u32[]{:S(2)}) async-start(f32[4,2,1536]{2,0,1:T(4,128)} %bitcast.35), calls=%async_computation | async-start | bytes 98304 | tf_op jit(solution)/shard_map/all_to_all | solution.py:82
  94.0 37.3 %collective-permute-start.3 = (bf16[6,9,1,3072]{3,0,2,1:T(8,128)(2,1)S(1)}, bf16[6,9,1,3072]{3,0,2,1:T(8,128)(2,1)S(1)}, u32[]{:S(2)}, u32[]{:S(2)}) collective-permute-start(bf16[6,9,1,3072]{3,0,2,1:T(8,128)(2,1)S(1)} %copy.106), channel_id=1, source_target_pairs={{1,0},{3,2},{5,4},{7,6},{9,8},{11,10},{13,12},{15,14},{17,16},{19,... | collective-permute-start | bytes 995336 | tf_op jit(solution)/shard_map/ppermute | solution.py:29
  95.5 36.1 %collective-permute-start.2 = (bf16[6,9,1,3072]{3,0,2,1:T(8,128)(2,1)S(1)}, bf16[6,9,1,3072]{3,0,2,1:T(8,128)(2,1)S(1)}, u32[]{:S(2)}, u32[]{:S(2)}) collective-permute-start(bf16[6,9,1,3072]{3,0,2,1:T(8,128)(2,1)S(1)} %copy.105), channel_id=1, source_target_pairs={{0,1},{2,3},{4,5},{6,7},{8,9},{10,11},{12,13},{14,15},{16,17},{18,... | collective-permute-start | bytes 995336 | tf_op jit(solution)/shard_map/ppermute | solution.py:27
  116.5 7.6 %all-to-all-start.1 = ((f32[2,8,1,1536]{3,0,2,1:T(2,128)}), f32[2,8,1,1536]{3,0,2,1:T(2,128)S(1)}, u32[]{:S(2)}, u32[]{:S(2)}) async-start(f32[2,8,1,1536]{3,0,2,1:T(2,128)} %copy.78), calls=%async_computation.1 | async-start | bytes 196608 | tf_op jit(solution)/shard_map/all_to_all | solution.py:93
  131.8 6.0 %copy-start.1 = (f32[6,4,3072]{2,1,0:T(4,128)S(1)}, f32[6,4,3072]{2,1,0:T(4,128)}, u32[]{:S(2)}) copy-start(f32[6,4,3072]{2,1,0:T(4,128)} %get-tuple-element.25) | copy-start | bytes 884740
  131.8 6.0 %copy-start.2 = (f32[6,4,3072]{2,1,0:T(4,128)S(1)}, f32[6,4,3072]{2,1,0:T(4,128)}, u32[]{:S(2)}) copy-start(f32[6,4,3072]{2,1,0:T(4,128)} %get-tuple-element.26) | copy-start | bytes 884740
  131.8 6.0 %copy-start.3 = (f32[6,4,3072]{2,1,0:T(4,128)S(1)}, f32[6,4,3072]{2,1,0:T(4,128)}, u32[]{:S(2)}) copy-start(f32[6,4,3072]{2,1,0:T(4,128)} %get-tuple-element.27) | copy-start | bytes 884740
  131.8 6.0 %copy-start.6 = (f32[4,3072]{1,0:T(4,128)S(1)}, f32[4,3072]{1,0:T(4,128)}, u32[]{:S(2)}) copy-start(f32[4,3072]{1,0:T(4,128)} %convert_multiply_fusion) | copy-start | bytes 147460
  131.8 6.0 %copy-start.9 = (bf16[1,1,9,9]{3,0,2,1:T(2,128)(2,1)S(1)}, bf16[1,1,9,9]{3,0,2,1:T(2,128)(2,1)}, u32[]{:S(2)}) copy-start(bf16[1,1,9,9]{3,0,2,1:T(2,128)(2,1)} %get-tuple-element.15) | copy-start | bytes 490
  131.8 6.0 %copy-start.10 = (f32[6,9]{1,0:T(8,128)S(1)}, f32[6,9]{1,0:T(8,128)}, u32[]{:S(2)}) copy-start(f32[6,9]{1,0:T(8,128)} %get-tuple-element.40) | copy-start | bytes 652
  131.8 6.0 %copy-start.11 = (f32[6,9]{1,0:T(8,128)S(1)}, f32[6,9]{1,0:T(8,128)}, u32[]{:S(2)}) copy-start(f32[6,9]{1,0:T(8,128)} %get-tuple-element.41) | copy-start | bytes 652
  131.8 6.0 %copy-start.12 = (pred[3072]{0:T(1024)(128)(4,1)S(1)}, pred[3072]{0:T(1024)(128)(4,1)}, u32[]{:S(2)}) copy-start(pred[3072]{0:T(1024)(128)(4,1)} %get-tuple-element.42) | copy-start | bytes 9220
  131.8 6.0 %copy-start.13 = (pred[3072]{0:T(1024)(128)(4,1)S(1)}, pred[3072]{0:T(1024)(128)(4,1)}, u32[]{:S(2)}) copy-start(pred[3072]{0:T(1024)(128)(4,1)} %get-tuple-element.43) | copy-start | bytes 9220
  131.8 6.0 %copy-start.14 = (f32[6]{0:T(128)S(1)}, f32[6]{0:T(128)}, u32[]{:S(2)}) copy-start(f32[6]{0:T(128)} %get-tuple-element.23) | copy-start | bytes 76
  131.9 6.0 %copy-start.15 = (f32[6,9]{1,0:T(8,128)S(1)}, f32[6,9]{1,0:T(8,128)}, u32[]{:S(2)}) copy-start(f32[6,9]{1,0:T(8,128)} %param.15) | copy-start | bytes 652
where the time goes:
time: 161 us; the launch traced here: 160 us
  blocking collectives  72 us (45%)
  matrix products  41 us (25%)
  local copies, waits for them, and re-layouts  18 us (11%)
  starting transfers between devices  17.6 us (11%)
  other arithmetic  9.11 us (6%)
    psum x1, blocking collectives, local(): summed = lax.psum(partial_modes, 'energy')  72 us
    dot_general x6, matrix products, harmonic_mix(): jnp.einsum('hk,ekxc->ehxc', matrix, values, preferred_element_type=jnp.fl...  36.6 us
    ppermute x2, starting transfers between devices, extended(): lax.ppermute(tail, axis, [(i, (i + 1) % count) for i in range(ends)])  8.23 us
    unnamed x36, local copies, waits for them, and re-layouts  6.2 us
    all_to_all x1, starting transfers between devices, solve_pencil(): lax.all_to_all(stacked, 'space', split_axis=1, concat_axis=2, tiled=True)  3.52 us
    add x1, other arithmetic, local(): doping + jnp.where(region_map == region, doping_levels[region], 0.0)  3.36 us
    all_to_all x1, starting transfers between devices, solve_pencil(): lax.all_to_all(blocks, 'space', split_axis=1, concat_axis=0, tiled=True)  3.28 us
  transfers between devices with their start and end apart: 6, of which 1 were waited for; matrix products, arithmetic and copies ran while one was open for 28% of the time, Pallas kernels for 0%

commit v1 on v0

v1 whole, which is shorter than its diff:
```python
import functools
import math

import jax
import jax.numpy as jnp
import numpy as np
from jax import lax
from jax.experimental import pallas as pl
from jax.experimental.pallas import tpu as pltpu
from jax.sharding import PartitionSpec as P

Y = 64
Z = 48
step_time = 0.4
contact_rate = 2.0
highest = lax.Precision.HIGHEST
MESH = pl.DeviceIdType.MESH
LANE = 128
GROUP = math.lcm(Z, LANE)
PER = GROUP // Z


def round_up(value, unit):
    return -(-value // unit) * unit


def sine(count):
    index = np.arange(count) + 1.0
    return math.sqrt(2.0 / (count + 1)) * np.sin(math.pi * np.outer(index, index) / (count + 1))


def eigen(count):
    return 2.0 - 2.0 * np.cos(math.pi * (np.arange(count) + 1.0) / (count + 1))


def tables(levels, harmonics, rows, energy, space):
    f32 = np.float32
    count = levels * harmonics * rows
    padded = round_up(count, 16)
    edge_count = levels * harmonics
    edge = round_up(edge_count, 16)
    r = np.arange(count)
    re, rh, rx = r // (harmonics * rows), (r // rows) % harmonics, r % rows
    s = np.arange(edge_count)
    se, sh = s // harmonics, s % harmonics
    pick = np.zeros((padded, LANE), f32)
    pick[r, rh] = 1
    pick_edge = np.zeros((LANE, 2 * edge), f32)
    pick_edge[sh, s] = 1
    pick_edge[sh, edge + s] = 1
    same_level = re[:, None] == re[None, :]
    masks = np.zeros((3, padded, padded), f32)
    ahead = (rx[None, :] == rx[:, None] + 1) * 0.5 - (rx[None, :] == rx[:, None] - 1) * 0.5
    masks[0, :count, :count] = same_level * ahead
    masks[1, :count, :count] = same_level * (rx[:, None] == rx[None, :]) * 0.5
    masks[2, :count, :count] = same_level * (rx[:, None] == rx[None, :])
    mask_edge = np.zeros((padded, 2 * edge), f32)
    mask_edge[:count, :edge_count] = -0.5 * (re[:, None] == se) * (rx[:, None] == 0)
    mask_edge[:count, edge : edge + edge_count] = 0.5 * (re[:, None] == se) * (rx[:, None] == rows - 1)
    choose = np.zeros((2 * edge, padded), f32)
    choose[s, s * rows] = 1
    choose[edge + s, s * rows + rows - 1] = 1
    dense = np.zeros((8, padded), f32)
    for x8 in range(rows):
        dense[x8, :count] = (rh == 0) & (rx == x8)
    eye = np.eye(padded, dtype=f32)

    groups = Y // PER
    block = Y // energy
    piece = round_up(block * rows, 8)
    total = rows * space
    theta = math.pi * (np.arange(Y) + 1.0) / (Y + 1)
    norm = math.sqrt(2.0 / (Y + 1))
    fc = np.zeros((energy * piece, groups * 8))
    fs = np.zeros((energy * piece, groups * 8))
    bc = np.zeros((groups * 8, energy * piece))
    bs = np.zeros((groups * 8, energy * piece))
    cos_in = np.zeros((energy * piece, GROUP))
    sin_in = np.zeros((energy * piece, GROUP))
    inner = np.repeat(np.arange(PER) + 1.0, Z)
    g = np.arange(groups)
    for j in range(Y):
        for x in range(rows):
            at = (j // block) * piece + (j % block) * rows + x
            cos_in[at], sin_in[at] = np.cos(inner * theta[j]), np.sin(inner * theta[j])
            ca, sa = norm * np.cos(PER * g * theta[j]), norm * np.sin(PER * g * theta[j])
            fc[at, g * 8 + x], fs[at, g * 8 + x] = ca, sa
            for copy in range(x, 8, rows):
                bc[g * 8 + copy, at], bs[g * 8 + copy, at] = ca, sa
    fold = np.zeros((GROUP, LANE))
    fold[:, :Z] = np.tile(sine(Z), (PER, 1))
    table = sine(total)
    into = np.zeros((block * total, space * piece))
    back = np.zeros((space, 2 * piece, block * total))
    field = np.zeros((total, total))
    for x in range(total):
        if x > 0:
            field[x] += 0.5 * table[x - 1]
        if x < total - 1:
            field[x] -= 0.5 * table[x + 1]
    lam = np.ones((energy, block * total, LANE))
    for jl in range(block):
        span = slice(jl * total, (jl + 1) * total)
        for sl in range(space):
            for x in range(rows):
                into[span, sl * piece + jl * rows + x] = table[sl * rows + x]
                back[sl, jl * rows + x, span] = table[sl * rows + x]
                back[sl, piece + jl * rows + x, span] = field[sl * rows + x]
        for q in range(energy):
            lam[q, span, :Z] = 1.0 / (
                eigen(total)[:, None] + eigen(Y)[q * block + jl] + eigen(Z)[None, :]
            )
    depth = np.arange(Y * Z) % Z
    zmask = np.zeros((2, 8, Y * Z))
    zmask[0] = depth > 0
    zmask[1] = depth < Z - 1
    values = dict(
        pick=pick, pick_t=pick.T, pick_edge=pick_edge, masks=masks, mask_edge=mask_edge,
        choose=choose, dense=dense, eye=eye, fc=fc, fs=fs, bc=bc, bs=bs, cos_in=cos_in,
        sin_in=sin_in, fold=fold, fold_t=fold.T, into=into, back=back, lam=lam, zmask=zmask,
    )
    values = {name: np.ascontiguousarray(value, f32) for name, value in values.items()}
    for name in ("choose",):
        values[name] = values[name].astype(jnp.bfloat16)
    return values


def dot32(a, b):
    return jnp.dot(a, b, precision=highest, preferred_element_type=jnp.float32)


def dot16(a, b):
    return jnp.dot(a, b, preferred_element_type=jnp.float32)


def kernel(names, energy, space, rows, scale, *refs):
    c = dict(zip(names, refs))
    (state, region, contact, doping, coupling, coef) = refs[len(names) : len(names) + 6]
    out, potential = refs[len(names) + 6 : len(names) + 8]
    (above, below, edge_out, edge_in, mix, mix_edge, total, charge, folded, modes, got1, part,
     got2, answer, got3, field, contact8, ssem, rsem, esend, erecv, s1, r1, s2, r2, s3, r3) = refs[
        len(names) + 8 :
    ]
    padded, cells = above.shape
    edge = edge_in.shape[0] // 2
    piece = modes.shape[1]
    groups = cells // GROUP
    me = lax.axis_index("energy")
    slab = lax.axis_index("space")

    barrier = pltpu.get_barrier_semaphore()

    @pl.loop(1, energy)
    def _(o):
        pl.semaphore_signal(
            barrier, inc=1, device_id={"energy": lax.rem(me + o, energy)}, device_id_type=MESH
        )

    @pl.loop(1, space)
    def _(o):
        pl.semaphore_signal(
            barrier, inc=1, device_id={"space": lax.rem(slab + o, space)}, device_id_type=MESH
        )

    pl.semaphore_wait(barrier, energy + space - 2)

    def lanes(g):
        return pl.ds(pl.multiple_of(g * GROUP, LANE), GROUP)

    def inside(g):
        return pl.ds(pl.multiple_of(g * GROUP + LANE, LANE), GROUP)

    def level_copy(g, up):
        target = jnp.minimum(me + 1, energy - 1) if up else jnp.maximum(me - 1, 0)
        return pltpu.make_async_remote_copy(
            src_ref=state.at[:, inside(g)],
            dst_ref=(below if up else above).at[:, lanes(g)],
            send_sem=ssem.at[int(up), g],
            recv_sem=rsem.at[int(up), g],
            device_id={"energy": target},
            device_id_type=MESH,
        )

    @pl.loop(0, groups)
    def _(g):
        @pl.when(me < energy - 1)
        def _():
            level_copy(g, True).start()

        @pl.when(me > 0)
        def _():
            level_copy(g, False).start()

    weight = dot32(c["dense"][...], coef[:, 2:3] * c["eye"][...]) * scale
    high = weight.astype(jnp.bfloat16)
    rest = weight - high.astype(jnp.float32)
    middle = rest.astype(jnp.bfloat16)
    low = (rest - middle.astype(jnp.float32)).astype(jnp.bfloat16)
    weights = jnp.concatenate([high, middle], axis=0)
    weights_low = jnp.concatenate([low, jnp.zeros_like(low)], axis=0)
    mine = jnp.where(me == 0, 1.0, 0.0).astype(jnp.float32)

    charge[...] = jnp.zeros_like(charge)
    for first in range(0, 8, rows):
        contact8[first : first + rows, :] = contact[...].astype(jnp.float32)
    found = jnp.zeros(region.shape, jnp.float32)
    for kind in range(doping.shape[0]):
        found = found + jnp.where(region[...] == kind, doping[kind], 0.0)
    charge[0:rows, :] = -found * mine
    choose = c["choose"][...]
    for g in range(groups):
        span = slice(g * GROUP, (g + 1) * GROUP)
        block = state[:, g * GROUP + LANE : (g + 1) * GROUP + LANE]
        parts = dot16(weights, block)
        fine = dot16(weights_low, block)
        folded[g * 8 : (g + 1) * 8, :] = parts[0:8] + (parts[8:16] + fine[0:8]) + charge[:, span]
        edge_out[:, span] = dot16(choose, block).astype(jnp.bfloat16)

    def edge_copy(up):
        target = jnp.minimum(slab + 1, space - 1) if up else jnp.maximum(slab - 1, 0)
        src = pl.ds(edge, edge) if up else pl.ds(0, edge)
        dst = pl.ds(0, edge) if up else pl.ds(edge, edge)
        return pltpu.make_async_remote_copy(
            src_ref=edge_out.at[src],
            dst_ref=edge_in.at[dst],
            send_sem=esend.at[int(up)],
            recv_sem=erecv.at[int(up)],
            device_id={"space": target},
            device_id_type=MESH,
        )

    charges = folded[...]
    turned = c["sin_in"][...] * dot32(c["fc"][...], charges) + c["cos_in"][...] * dot32(
        c["fs"][...], charges
    )
    modes[...] = dot32(turned, c["fold"][...]).reshape(modes.shape)

    def spread(source, fixed, got, sends, recvs, o, sending):
        other = lax.rem(me + o, energy) if sending else lax.rem(me + energy - o, energy)
        return pltpu.make_async_remote_copy(
            src_ref=source if fixed else source.at[other],
            dst_ref=got.at[me if sending else other],
            send_sem=sends.at[o],
            recv_sem=recvs.at[me if sending else other],
            device_id={"energy": other},
            device_id_type=MESH,
        )

    @pl.loop(1, energy)
    def _(o):
        spread(modes, False, got1, s1, r1, o, True).start()

    @pl.when(slab < space - 1)
    def _():
        edge_copy(True).start()

    @pl.when(slab > 0)
    def _():
        edge_copy(False).start()

    pick, pick_t = c["pick"][...], c["pick_t"][...]
    for d in range(6):
        wide = dot16(pick, coupling[d])
        mask = c["masks"][0 if d == 0 else 1 if d < 3 else 2]
        mix[d] = (dot16(wide, pick_t) * mask).astype(jnp.bfloat16)
        if d == 0:
            mix_edge[...] = (dot16(wide, c["pick_edge"][...]) * c["mask_edge"][...]).astype(
                jnp.bfloat16
            )

    speed = step_time * coef[:, 0:1]
    pull = (step_time * 3.0) * coef[:, 1:2]
    rate_up = step_time * coef[:, 3:4]
    rate_down = step_time * coef[:, 4:5]
    plain = 1.0 / (1.0 + step_time * coef[:, 5:6])
    held = 1.0 / (1.0 + step_time * (coef[:, 5:6] + contact_rate)) - plain

    @pl.loop(0, groups)
    def _(g):
        block = state[:, inside(g)]
        around = state[:, pl.ds(pl.multiple_of(g * GROUP, LANE), GROUP + 2 * LANE)]
        size = GROUP + 2 * LANE
        ty = dot16(mix[1], around)
        ty = (pltpu.roll(ty, size - Z, axis=1) - pltpu.roll(ty, Z, axis=1))[:, LANE : LANE + GROUP]
        tz = dot16(mix[2], block)
        tz = pltpu.roll(tz, GROUP - 1, axis=1) * c["zmask"][1, 0:1, 0:GROUP] - pltpu.roll(
            tz, 1, axis=1
        ) * c["zmask"][0, 0:1, 0:GROUP]
        total[:, lanes(g)] = block.astype(jnp.float32) - speed * (dot16(mix[0], block) + ty + tz)

    @pl.loop(1, energy)
    def _(o):
        spread(modes, False, got1, s1, r1, o, False).wait_recv()

    got1[me] = modes[me]
    summed = got1[0]
    for q in range(1, energy):
        summed = summed + got1[q]
    part[...] = summed

    def pencil(o, sending):
        other = lax.rem(slab + o, space) if sending else lax.rem(slab + space - o, space)
        return pltpu.make_async_remote_copy(
            src_ref=part,
            dst_ref=got2.at[slab if sending else other],
            send_sem=s2.at[o],
            recv_sem=r2.at[slab if sending else other],
            device_id={"space": other},
            device_id_type=MESH,
        )

    @pl.loop(1, space)
    def _(o):
        pencil(o, True).start()

    got2[slab] = part[...]

    @pl.loop(1, space)
    def _(o):
        pencil(o, False).wait_recv()

    spectral = dot32(c["into"][...], got2[...].reshape(space * piece, LANE)) * c["lam"][me]
    answer[...] = dot32(c["back"][slab], spectral)

    @pl.loop(1, energy)
    def _(o):
        spread(answer, True, got3, s3, r3, o, True).start()

    got3[me] = answer[...]

    @pl.loop(1, energy)
    def _(o):
        spread(answer, True, got3, s3, r3, o, False).wait_recv()

    for which in range(2):
        lines = got3[:, which * piece : (which + 1) * piece, :].reshape(energy * piece, LANE)
        lines = dot32(lines, c["fold_t"][...])
        lines = dot32(c["bs"][...], c["cos_in"][...] * lines) + dot32(
            c["bc"][...], c["sin_in"][...] * lines
        )
        for g in range(groups):
            span = slice(g * GROUP, (g + 1) * GROUP)
            if which == 0:
                charge[:, span] = lines[g * 8 : (g + 1) * 8]
            else:
                field[0, :, span] = lines[g * 8 : (g + 1) * 8]
    level = charge[...]
    potential[...] = level[0:rows]
    column = lax.broadcasted_iota(jnp.int32, level.shape, 1)
    field[1] = 0.5 * (
        jnp.where(column >= Z, pltpu.roll(level, Z, axis=1), 0.0)
        - jnp.where(column < cells - Z, pltpu.roll(level, cells - Z, axis=1), 0.0)
    )
    field[2] = 0.5 * (
        c["zmask"][0] * pltpu.roll(level, 1, axis=1)
        - c["zmask"][1] * pltpu.roll(level, cells - 1, axis=1)
    )

    @pl.when(slab > 0)
    def _():
        edge_copy(True).wait_recv()

    @pl.when(slab == 0)
    def _():
        edge_in[0:edge, :] = jnp.zeros((edge, cells), jnp.bfloat16)

    @pl.when(slab < space - 1)
    def _():
        edge_copy(False).wait_recv()

    @pl.when(slab == space - 1)
    def _():
        edge_in[edge : 2 * edge, :] = jnp.zeros((edge, cells), jnp.bfloat16)

    @pl.when(me == 0)
    def _():
        below[...] = jnp.zeros_like(below)

    @pl.when(me == energy - 1)
    def _():
        above[...] = jnp.zeros_like(above)

    def over(values):
        return values.reshape(padded // 8, 8, GROUP)

    @pl.loop(0, groups)
    def _(g):
        block = state[:, inside(g)]
        pulled = over(dot16(mix[3], block)) * field[0, :, lanes(g)][None]
        pulled = pulled + over(dot16(mix[4], block)) * field[1, :, lanes(g)][None]
        pulled = pulled + over(dot16(mix[5], block)) * field[2, :, lanes(g)][None]
        total[:, lanes(g)] = (
            total[:, lanes(g)]
            + pull * pulled.reshape(padded, GROUP)
            - speed * dot16(mix_edge[...], edge_in[:, lanes(g)])
        )

    @pl.loop(0, groups)
    def _(g):
        @pl.when(me > 0)
        def _():
            level_copy(g, True).wait_recv()

        @pl.when(me < energy - 1)
        def _():
            level_copy(g, False).wait_recv()

        value = (
            total[:, lanes(g)]
            + rate_up * above[:, lanes(g)].astype(jnp.float32)
            + rate_down * below[:, lanes(g)].astype(jnp.float32)
        )
        spots = jnp.broadcast_to(
            contact8[:, lanes(g)][None], (padded // 8, 8, GROUP)
        ).reshape(padded, GROUP)
        out[:, lanes(g)] = (value * (plain + held * spots)).astype(jnp.bfloat16)

    @pl.loop(0, groups)
    def _(g):
        @pl.when(me < energy - 1)
        def _():
            level_copy(g, True).wait_send()

        @pl.when(me > 0)
        def _():
            level_copy(g, False).wait_send()

    @pl.loop(1, energy)
    def _(o):
        spread(modes, False, got1, s1, r1, o, True).wait_send()
        spread(answer, True, got3, s3, r3, o, True).wait_send()

    @pl.loop(1, space)
    def _(o):
        pencil(o, True).wait_send()

    @pl.when(slab < space - 1)
    def _():
        edge_copy(True).wait_send()

    @pl.when(slab > 0)
    def _():
        edge_copy(False).wait_send()


def local(
    energy,
    space,
    distribution,
    region_map,
    contact_mask,
    doping_levels,
    coupling,
    level_coef,
    phonon_kernel,
    out_rate,
):
    levels, harmonics, rows, cells = distribution.shape
    count = levels * harmonics * rows
    padded = round_up(count, 16)
    edge = round_up(levels * harmonics, 16)
    constants = tables(levels, harmonics, rows, energy, space)
    names = tuple(constants)
    piece = round_up(Y // energy * rows, 8)
    groups = cells // GROUP
    state = jnp.pad(
        distribution.reshape(count, cells), ((0, padded - count), (LANE, LANE))
    )
    shape = (levels, harmonics, rows)
    coef = jnp.stack(
        [jnp.broadcast_to(level_coef[:, i][:, None, None], shape) for i in range(3)]
        + [jnp.broadcast_to(phonon_kernel[i][:, :, None], shape) for i in range(2)]
        + [jnp.broadcast_to(out_rate[:, :, None], shape)],
        axis=-1,
    ).reshape(count, 6)
    coef = jnp.pad(coef, ((0, padded - count), (0, 2)))
    wide = jnp.pad(
        coupling.reshape(6, harmonics, harmonics).astype(jnp.float32),
        ((0, 0), (0, LANE - harmonics), (0, LANE - harmonics)),
    )
    vmem = pl.BlockSpec(memory_space=pltpu.VMEM)
    smem = pl.BlockSpec(memory_space=pltpu.SMEM)
    bf16, f32 = jnp.bfloat16, jnp.float32
    dma = pltpu.SemaphoreType.DMA
    out, potential = pl.pallas_call(
        functools.partial(
            kernel, names, energy, space, rows, 1.0 / math.sqrt(levels * energy)
        ),
        out_shape=(
            jax.ShapeDtypeStruct((padded, cells), bf16),
            jax.ShapeDtypeStruct((rows, cells), f32),
        ),
        in_specs=[vmem] * (len(names) + 3) + [smem] + [vmem] * 2,
        out_specs=(vmem, vmem),
        scratch_shapes=[
            pltpu.VMEM((padded, cells), bf16),
            pltpu.VMEM((padded, cells), bf16),
            pltpu.VMEM((2 * edge, cells), bf16),
            pltpu.VMEM((2 * edge, cells), bf16),
            pltpu.VMEM((6, padded, padded), bf16),
            pltpu.VMEM((padded, 2 * edge), bf16),
            pltpu.VMEM((padded, cells), f32),
            pltpu.VMEM((8, cells), f32),
            pltpu.VMEM((groups * 8, GROUP), f32),
            pltpu.VMEM((energy, piece, LANE), f32),
            pltpu.VMEM((energy, piece, LANE), f32),
            pltpu.VMEM((piece, LANE), f32),
            pltpu.VMEM((space, piece, LANE), f32),
            pltpu.VMEM((2 * piece, LANE), f32),
            pltpu.VMEM((energy, 2 * piece, LANE), f32),
            pltpu.VMEM((3, 8, cells), f32),
            pltpu.VMEM((8, cells), f32),
            dma((2, groups)),
            dma((2, groups)),
            dma((2,)),
            dma((2,)),
            dma((energy,)),
            dma((energy,)),
            dma((space,)),
            dma((space,)),
            dma((energy,)),
            dma((energy,)),
        ],
        compiler_params=pltpu.CompilerParams(
            collective_id=0, has_side_effects=True, vmem_limit_bytes=48 * 1024 * 1024
        ),
        cost_estimate=pl.CostEstimate(
            flops=2 * 7 * padded * padded * cells,
            bytes_accessed=8 * padded * cells,
            transcendentals=0,
        ),
    )(
        *[jnp.asarray(constants[name]) for name in names],
        state,
        region_map,
        contact_mask,
        doping_levels,
        wide,
        coef,
    )
    return out[:count].reshape(distribution.shape), potential


def solution(mesh):
    return jax.shard_map(
        functools.partial(local, mesh.shape["energy"], mesh.shape["space"]),
        mesh=mesh,
        in_specs=(
            P("energy", None, "space", None),
            P("space", None),
            P("space", None),
            P(),
            P(),
            P("energy", None),
            P(None, "energy", None),
            P("energy", None),
        ),
        out_specs=(P("energy", None, "space", None), P("space", None)),
        check_vma=False,
    )
```

time: 161 us -> 69.3 us (0.43)
  the two profiles are of different devices: /device:TPU:0 before, /device:TPU:4 now
where the time goes in v1:
time: 69.3 us; the launch traced here: 68.1 us
  Pallas kernels  55.9 us (81%)
  local copies, waits for them, and re-layouts  11.1 us (16%)
  between operations  1 us (1%)
    pallas_call x1, Pallas kernels, local(): pl.pallas_call(functools.partial(kernel, names, energy, space, rows, 1.0...  55.9 us
    reshape x1, local copies, waits for them, and re-layouts, local(): distribution.reshape(count, cells)  2.67 us
    another operation x8, local copies, waits for them, and re-layouts, local(): jnp.stack([jnp.broadcast_to(level_coef[:, i][:, None, None], shape) for i...  2.57 us
    unnamed x48, local copies, waits for them, and re-layouts  2.25 us
    reshape x1, local copies, waits for them, and re-layouts, local(): return (out[:count].reshape(distribution.shape), potential)  1.54 us

profile of v1, /device:TPU:4, one launch (start us, length us, event | category | flops | bytes accessed | tf_op | source)
XLA Modules:
  0.0 68.1 jit_solution(13186766025650344991)
XLA Ops:
  0.6 0.8 %slice_bitcast_fusion = (f32[6]{0:T(128)S(1)}, f32[6]{0:T(128)S(1)}, f32[6]{0:T(128)S(1)}) fusion(f32[6,3]{0,1:T(4,128)} %param.33), kind=kLoop, calls=%fused_computation.3 | loop fusion | bytes 144 | tf_op jit(solution)/shard_map/stack;broadcast_in_dim | solution.py:470
  1.4 0.8 %fusion = (f32[1,6,9]{2,0,1:T(1,128)S(1)}, f32[1,6,9]{2,0,1:T(1,128)S(1)}) fusion(f32[2,6,9]{2,0,1:T(2,128)} %param.34), kind=kLoop, calls=%fused_computation.6 | loop fusion | bytes 864 | tf_op jit(solution)/shard_map/slice | solution.py:472
  2.2 0.7 %copy.30 = bf16[2,3,9,9]{3,2,1,0:T(8,128)(2,1)S(1)} copy(bf16[2,3,9,9]{3,0,2,1:T(2,128)(2,1)} %param.32) | data formatting | bytes 1944 | tf_op args[4]
  2.9 0.1 stack_broadcast_in_dim.43
  3.0 0.1 stack_broadcast_in_dim.41
  3.1 0.1 stack_broadcast_in_dim.42
  3.3 0.1 stack_broadcast_in_dim.37
  3.3 0.1 stack_broadcast_in_dim.39
  3.4 0.8 %stack_broadcast_in_dim.44 = f32[6,9,4,1]{3,2,1,0:T(4,128)S(1)} broadcast(f32[6,9]{1,0:T(8,128)} %param.35), dimensions={0,1} | broadcast | bytes 1080 | tf_op jit(solution)/shard_map/stack;broadcast_in_dim | solution.py:470
  4.2 0.5 stack.3
  4.8 0.0 copy-start.12
  4.8 0.0 copy-start.13
  4.8 0.0 copy-start.14
  4.8 0.0 copy-start.15
  4.9 0.0 copy-start.16
  4.9 0.0 copy-start.17
  4.9 0.0 copy-start.18
  4.9 0.0 copy-start.19
  4.9 0.0 copy-start.21
  4.9 0.0 copy-start.22
  4.9 2.7 %reshape.30 = bf16[216,3072]{1,0:T(8,128)(2,1)S(1)} reshape(bf16[6,9,4,3072]{3,2,1,0:T(4,128)(2,1)} %param.28) | data formatting | bytes 2654208 | tf_op jit(solution)/shard_map/reshape | solution.py:467
  7.6 0.0 copy-start
  7.6 0.0 copy-start.1
  7.6 0.0 copy-start.2
  7.6 0.0 copy-start.3
  7.7 0.0 copy-start.4
  7.7 0.0 copy-start.5
  7.7 0.0 copy-start.6
  7.7 0.0 copy-start.7
  7.7 0.0 copy-start.8
  7.7 0.0 copy-start.9
  7.7 0.0 copy-start.10
  7.7 0.0 copy-start.11
  7.8 0.0 copy-start.20
  7.8 1.2 %pad.14.refs_20_ = bf16[224,3328]{1,0:T(8,128)(2,1)} pad(bf16[216,3072]{1,0:T(8,128)(2,1)S(1)} %reshape.30, bf16[]{:T(256)} %constant.44.clone.1), padding=0_8x128_128 | pad | bytes 2818050 | tf_op jit(solution)/shard_map/jit(_pad)/pad | solution.py:466
  9.0 0.0 copy-done.15
  9.1 0.0 copy-done.4
  9.2 0.4 copy-done.5
  9.5 0.1 copy-done.6
  9.6 0.1 copy-done.7
  9.7 0.1 copy-done.8
  9.7 0.1 copy-done.9
  9.8 0.1 copy-done.10
  9.9 0.0 copy-done.11
  9.9 55.9 %shard_map.275 = (bf16[224,3072]{1,0:T(8,128)(2,1)S(1)}, f32[4,3072]{1,0:T(4,128)S(1)}) custom-call(f32[224,128]{1,0:T(8,128)S(1)} %copy-done.15, f32[128,224]{1,0:T(8,128)S(1)} %copy-done.13, f32[128,128]{1,0:T(8,128)S(1)} %copy-done.19, f32[3,224,224]{2,1,0:T(8,128)S(1)} %copy-done.3, f32[224,128]{1,0:T(8,128)S(1)} %copy-done.14, ...), custom_call_target="tpu_custom_call" | custom-call | flops 2157969408 | bytes 5505024 | tf_op jit(solution)/shard_map/pallas_call | solution.py:485
  65.9 0.1 slice.23
  66.0 1.5 %reshape.32 = bf16[6,9,4,3072]{3,2,1,0:T(4,128)(2,1)} reshape(bf16[216,3072]{1,0:T(8,128)(2,1)S(1)} %slice.23) | data formatting | bytes 2654208 | tf_op jit(solution)/shard_map/reshape | solution.py:541
  67.5 0.6 copy.38
  (17 shorter events, 0.1 us)
Async XLA Ops:
  4.8 4.2 %copy-start.12 = (f32[256,64]{1,0:T(8,128)S(1)}, f32[256,64]{1,0:T(8,128)}, u32[]{:S(2)}) copy-start(f32[256,64]{1,0:T(8,128)} %constant.54.clone.refs_8_) | copy-start | bytes 196612
  4.8 4.2 %copy-start.13 = (f32[128,224]{1,0:T(8,128)S(1)}, f32[128,224]{1,0:T(8,128)}, u32[]{:S(2)}) copy-start(f32[128,224]{1,0:T(8,128)} %constant.47.clone.refs_1_) | copy-start | bytes 344068
  4.8 4.2 %copy-start.14 = (f32[224,128]{1,0:T(8,128)S(1)}, f32[224,128]{1,0:T(8,128)}, u32[]{:S(2)}) copy-start(f32[224,128]{1,0:T(8,128)} %constant.50.clone.refs_4_) | copy-start | bytes 344068
  4.8 4.2 %copy-start.15 = (f32[224,128]{1,0:T(8,128)S(1)}, f32[224,128]{1,0:T(8,128)}, u32[]{:S(2)}) copy-start(f32[224,128]{1,0:T(8,128)} %constant.46.clone.refs_0_) | copy-start | bytes 344068
  4.9 4.2 %copy-start.16 = (f32[64,256]{1,0:T(8,128)S(1)}, f32[64,256]{1,0:T(8,128)}, u32[]{:S(2)}) copy-start(f32[64,256]{1,0:T(8,128)} %constant.57.clone.refs_11_) | copy-start | bytes 196612
  4.9 4.2 %copy-start.17 = (f32[64,256]{1,0:T(8,128)S(1)}, f32[64,256]{1,0:T(8,128)}, u32[]{:S(2)}) copy-start(f32[64,256]{1,0:T(8,128)} %constant.56.clone.refs_10_) | copy-start | bytes 196612
  4.9 4.2 %copy-start.18 = (bf16[128,224]{1,0:T(8,128)(2,1)S(1)}, bf16[128,224]{1,0:T(8,128)(2,1)}, u32[]{:S(2)}) copy-start(bf16[128,224]{1,0:T(8,128)(2,1)} %constant.51.clone.refs_5_) | copy-start | bytes 172036
  4.9 4.2 %copy-start.19 = (f32[128,128]{1,0:T(8,128)S(1)}, f32[128,128]{1,0:T(8,128)}, u32[]{:S(2)}) copy-start(f32[128,128]{1,0:T(8,128)} %constant.48.clone.refs_2_) | copy-start | bytes 196612
  4.9 4.2 %copy-start.21 = (f32[32,32]{1,0:T(8,128)S(1)}, f32[32,32]{1,0:T(8,128)}, u32[]{:S(2)}) copy-start(f32[32,32]{1,0:T(8,128)} %constant.62.clone.refs_16_) | copy-start | bytes 12292
  4.9 4.2 %copy-start.22 = (f32[8,224]{1,0:T(8,128)S(1)}, f32[8,224]{1,0:T(8,128)}, u32[]{:S(2)}) copy-start(f32[8,224]{1,0:T(8,128)} %constant.52.clone.refs_6_) | copy-start | bytes 21508
  7.6 1.5 %copy-start = (s32[4,3072]{1,0:T(4,128)S(1)}, s32[4,3072]{1,0:T(4,128)}, u32[]{:S(2)}) copy-start(s32[4,3072]{1,0:T(4,128)} %refs_21_.1) | copy-start | bytes 147460
  7.6 1.5 %copy-start.1 = (s32[4,3072]{1,0:T(4,128)S(1)}, s32[4,3072]{1,0:T(4,128)}, u32[]{:S(2)}) copy-start(s32[4,3072]{1,0:T(4,128)} %refs_22_.1) | copy-start | bytes 147460
  7.6 1.5 %copy-start.2 = (f32[4]{0:T(128)S(1)}, f32[4]{0:T(128)}, u32[]{:S(2)}) copy-start(f32[4]{0:T(128)} %refs_23_.1) | copy-start | bytes 52
  7.6 1.5 %copy-start.3 = (f32[3,224,224]{2,1,0:T(8,128)S(1)}, f32[3,224,224]{2,1,0:T(8,128)}, u32[]{:S(2)}) copy-start(f32[3,224,224]{2,1,0:T(8,128)} %constant.49.clone.refs_3_) | copy-start | bytes 1806340
  7.7 1.5 %copy-start.4 = (f32[256,384]{1,0:T(8,128)S(1)}, f32[256,384]{1,0:T(8,128)}, u32[]{:S(2)}) copy-start(f32[256,384]{1,0:T(8,128)} %constant.59.clone.refs_13_) | copy-start | bytes 1179652
  7.7 1.9 %copy-start.5 = (f32[256,384]{1,0:T(8,128)S(1)}, f32[256,384]{1,0:T(8,128)}, u32[]{:S(2)}) copy-start(f32[256,384]{1,0:T(8,128)} %constant.58.clone.refs_12_) | copy-start | bytes 1179652
  7.7 1.9 %copy-start.6 = (f32[16,32,128]{2,1,0:T(8,128)S(1)}, f32[16,32,128]{2,1,0:T(8,128)}, u32[]{:S(2)}) copy-start(f32[16,32,128]{2,1,0:T(8,128)} %constant.64.clone.refs_18_) | copy-start | bytes 786436
  7.7 2.0 %copy-start.7 = (f32[224,224]{1,0:T(8,128)S(1)}, f32[224,224]{1,0:T(8,128)}, u32[]{:S(2)}) copy-start(f32[224,224]{1,0:T(8,128)} %constant.53.clone.refs_7_) | copy-start | bytes 602116
  7.7 2.0 %copy-start.8 = (f32[2,8,3072]{2,1,0:T(8,128)S(1)}, f32[2,8,3072]{2,1,0:T(8,128)}, u32[]{:S(2)}) copy-start(f32[2,8,3072]{2,1,0:T(8,128)} %constant.65.clone.refs_19_) | copy-start | bytes 589828
  7.7 2.1 %copy-start.9 = (f32[128,384]{1,0:T(8,128)S(1)}, f32[128,384]{1,0:T(8,128)}, u32[]{:S(2)}) copy-start(f32[128,384]{1,0:T(8,128)} %constant.61.clone.refs_15_) | copy-start | bytes 589828
  7.7 2.1 %copy-start.10 = (f32[384,128]{1,0:T(8,128)S(1)}, f32[384,128]{1,0:T(8,128)}, u32[]{:S(2)}) copy-start(f32[384,128]{1,0:T(8,128)} %constant.60.clone.refs_14_) | copy-start | bytes 589828
  7.7 2.2 %copy-start.11 = (f32[256,64]{1,0:T(8,128)S(1)}, f32[256,64]{1,0:T(8,128)}, u32[]{:S(2)}) copy-start(f32[256,64]{1,0:T(8,128)} %constant.55.clone.refs_9_) | copy-start | bytes 196612
  7.8 2.1 %copy-start.20 = (f32[2,32,32]{2,1,0:T(8,128)S(1)}, f32[2,32,32]{2,1,0:T(8,128)}, u32[]{:S(2)}) copy-start(f32[2,32,32]{2,1,0:T(8,128)} %constant.63.clone.refs_17_) | copy-start | bytes 24580

commit v2 on v1

--- a/solution.py
+++ b/solution.py
@@ -43,9 +43,11 @@
     re, rh, rx = r // (harmonics * rows), (r // rows) % harmonics, r % rows
     s = np.arange(edge_count)
     se, sh = s // harmonics, s % harmonics
-    pick = np.zeros((padded, LANE), f32)
+    pick = np.zeros((padded, harmonics), f32)
     pick[r, rh] = 1
-    pick_edge = np.zeros((LANE, 2 * edge), f32)
+    pick_level = np.zeros((padded, levels), f32)
+    pick_level[r, re] = 1
+    pick_edge = np.zeros((harmonics, 2 * edge), f32)
     pick_edge[sh, s] = 1
     pick_edge[sh, edge + s] = 1
     same_level = re[:, None] == re[None, :]
@@ -63,7 +65,6 @@
     dense = np.zeros((8, padded), f32)
     for x8 in range(rows):
         dense[x8, :count] = (rh == 0) & (rx == x8)
-    eye = np.eye(padded, dtype=f32)
 
     groups = Y // PER
     block = Y // energy
@@ -88,7 +89,12 @@
             for copy in range(x, 8, rows):
                 bc[g * 8 + copy, at], bs[g * 8 + copy, at] = ca, sa
     fold = np.zeros((GROUP, LANE))
+    half = LANE // 2
     fold[:, :Z] = np.tile(sine(Z), (PER, 1))
+    fold[:, half : half + Z] = fold[:, :Z]
+    unfold = np.zeros((2, LANE, GROUP))
+    unfold[0, :Z] = fold[:, :Z].T
+    unfold[1, half : half + Z] = fold[:, :Z].T
     table = sine(total)
     into = np.zeros((block * total, space * piece))
     back = np.zeros((space, 2 * piece, block * total))
@@ -110,17 +116,19 @@
             lam[q, span, :Z] = 1.0 / (
                 eigen(total)[:, None] + eigen(Y)[q * block + jl] + eigen(Z)[None, :]
             )
+            lam[q, span, half : half + Z] = lam[q, span, :Z]
     depth = np.arange(Y * Z) % Z
     zmask = np.zeros((2, 8, Y * Z))
     zmask[0] = depth > 0
     zmask[1] = depth < Z - 1
     values = dict(
         pick=pick, pick_t=pick.T, pick_edge=pick_edge, masks=masks, mask_edge=mask_edge,
-        choose=choose, dense=dense, eye=eye, fc=fc, fs=fs, bc=bc, bs=bs, cos_in=cos_in,
-        sin_in=sin_in, fold=fold, fold_t=fold.T, into=into, back=back, lam=lam, zmask=zmask,
+        choose=choose, dense=dense, pick_level=pick_level,
+        pick_level_t=pick_level.T, fc=fc, fs=fs, bc=bc, bs=bs, cos_in=cos_in,
+        sin_in=sin_in, fold=fold, unfold=unfold, into=into, back=back, lam=lam, zmask=zmask,
     )
     values = {name: np.ascontiguousarray(value, f32) for name, value in values.items()}
-    for name in ("choose",):
+    for name in ("choose", "masks", "mask_edge"):
         values[name] = values[name].astype(jnp.bfloat16)
     return values
 
@@ -135,11 +143,13 @@
 
 def kernel(names, energy, space, rows, scale, *refs):
     c = dict(zip(names, refs))
-    (state, region, contact, doping, coupling, coef) = refs[len(names) : len(names) + 6]
-    out, potential = refs[len(names) + 6 : len(names) + 8]
-    (above, below, edge_out, edge_in, mix, mix_edge, total, charge, folded, modes, got1, part,
+    (given, region, contact, doping, coupling, level_coef, level_coef_t, phonon, out_rate) = refs[
+        len(names) : len(names) + 9
+    ]
+    out, potential = refs[len(names) + 9 : len(names) + 11]
+    (state, above, below, edge_out, edge_in, mix, mix_edge, total, pulls, charge, folded, modes, got1, part,
      got2, answer, got3, field, contact8, ssem, rsem, esend, erecv, s1, r1, s2, r2, s3, r3) = refs[
-        len(names) + 8 :
+        len(names) + 11 :
     ]
     padded, cells = above.shape
     edge = edge_in.shape[0] // 2
@@ -181,17 +191,32 @@
             device_id_type=MESH,
         )
 
+    def send_levels(first, last):
+        @pl.loop(first, last)
+        def _(g):
+            @pl.when(me < energy - 1)
+            def _():
+                level_copy(g, True).start()
+
+            @pl.when(me > 0)
+            def _():
+                level_copy(g, False).start()
+
+    state[:, 0:LANE] = jnp.zeros((padded, LANE), jnp.bfloat16)
+    state[:, cells + LANE :] = jnp.zeros((padded, LANE), jnp.bfloat16)
+    count = given.shape[0] * rows
+
     @pl.loop(0, groups)
     def _(g):
-        @pl.when(me < energy - 1)
-        def _():
-            level_copy(g, True).start()
-
-        @pl.when(me > 0)
-        def _():
-            level_copy(g, False).start()
-
-    weight = dot32(c["dense"][...], coef[:, 2:3] * c["eye"][...]) * scale
+        block = given[:, :, lanes(g)].astype(jnp.float32).reshape(count, GROUP)
+        block = jnp.concatenate([block, jnp.zeros((padded - count, GROUP), jnp.float32)], axis=0)
+        state[:, inside(g)] = block.astype(jnp.bfloat16)
+
+    first, second, third = groups // 4, groups // 2, groups * 5 // 8
+    send_levels(0, first)
+
+    density = dot32(level_coef_t[...], c["pick_level_t"][...])[2:3, :]
+    weight = c["dense"][...] * density * scale
     high = weight.astype(jnp.bfloat16)
     rest = weight - high.astype(jnp.float32)
     middle = rest.astype(jnp.bfloat16)
@@ -201,8 +226,8 @@
     mine = jnp.where(me == 0, 1.0, 0.0).astype(jnp.float32)
 
     charge[...] = jnp.zeros_like(charge)
-    for first in range(0, 8, rows):
-        contact8[first : first + rows, :] = contact[...].astype(jnp.float32)
+    for row in range(0, 8, rows):
+        contact8[row : row + rows, :] = contact[...].astype(jnp.float32)
     found = jnp.zeros(region.shape, jnp.float32)
     for kind in range(doping.shape[0]):
         found = found + jnp.where(region[...] == kind, doping[kind], 0.0)
@@ -250,30 +275,29 @@
     def _(o):
         spread(modes, False, got1, s1, r1, o, True).start()
 
-    @pl.when(slab < space - 1)
-    def _():
-        edge_copy(True).start()
-
-    @pl.when(slab > 0)
-    def _():
-        edge_copy(False).start()
+    send_levels(first, second)
 
     pick, pick_t = c["pick"][...], c["pick_t"][...]
     for d in range(6):
-        wide = dot16(pick, coupling[d])
-        mask = c["masks"][0 if d == 0 else 1 if d < 3 else 2]
+        wide = dot16(pick, coupling[d // 3, d % 3].astype(jnp.float32))
+        mask = c["masks"][0 if d == 0 else 1 if d < 3 else 2].astype(jnp.float32)
         mix[d] = (dot16(wide, pick_t) * mask).astype(jnp.bfloat16)
         if d == 0:
             mix_edge[...] = (dot16(wide, c["pick_edge"][...]) * c["mask_edge"][...]).astype(
                 jnp.bfloat16
             )
 
+    def by_row(values):
+        return jnp.sum(dot32(c["pick_level"][...], values) * pick, axis=1, keepdims=True)
+
+    coef = dot32(c["pick_level"][...], level_coef[...])
     speed = step_time * coef[:, 0:1]
     pull = (step_time * 3.0) * coef[:, 1:2]
-    rate_up = step_time * coef[:, 3:4]
-    rate_down = step_time * coef[:, 4:5]
-    plain = 1.0 / (1.0 + step_time * coef[:, 5:6])
-    held = 1.0 / (1.0 + step_time * (coef[:, 5:6] + contact_rate)) - plain
+    rate_up = step_time * by_row(phonon[0])
+    rate_down = step_time * by_row(phonon[1])
+    decay = by_row(out_rate[...])
+    plain = 1.0 / (1.0 + step_time * decay)
+    held = 1.0 / (1.0 + step_time * (decay + contact_rate)) - plain
 
     @pl.loop(0, groups)
     def _(g):
@@ -287,6 +311,8 @@
             tz, 1, axis=1
         ) * c["zmask"][0, 0:1, 0:GROUP]
         total[:, lanes(g)] = block.astype(jnp.float32) - speed * (dot16(mix[0], block) + ty + tz)
+        for d in range(3):
+            pulls[d, :, lanes(g)] = dot16(mix[3 + d], block)
 
     @pl.loop(1, energy)
     def _(o):
@@ -313,6 +339,16 @@
     def _(o):
         pencil(o, True).start()
 
+    send_levels(second, third)
+
+    @pl.when(slab < space - 1)
+    def _():
+        edge_copy(True).start()
+
+    @pl.when(slab > 0)
+    def _():
+        edge_copy(False).start()
+
     got2[slab] = part[...]
 
     @pl.loop(1, space)
@@ -320,12 +356,15 @@
         pencil(o, False).wait_recv()
 
     spectral = dot32(c["into"][...], got2[...].reshape(space * piece, LANE)) * c["lam"][me]
-    answer[...] = dot32(c["back"][slab], spectral)
+    both = dot32(c["back"][slab], spectral)
+    lower = lax.broadcasted_iota(jnp.int32, (piece, LANE), 1) < LANE // 2
+    answer[...] = jnp.where(lower, both[0:piece], both[piece:])
 
     @pl.loop(1, energy)
     def _(o):
         spread(answer, True, got3, s3, r3, o, True).start()
 
+    send_levels(third, groups)
     got3[me] = answer[...]
 
     @pl.loop(1, energy)
@@ -333,8 +372,7 @@
         spread(answer, True, got3, s3, r3, o, False).wait_recv()
 
     for which in range(2):
-        lines = got3[:, which * piece : (which + 1) * piece, :].reshape(energy * piece, LANE)
-        lines = dot32(lines, c["fold_t"][...])
+        lines = dot32(got3[...].reshape(energy * piece, LANE), c["unfold"][which])
         lines = dot32(c["bs"][...], c["cos_in"][...] * lines) + dot32(
             c["bc"][...], c["sin_in"][...] * lines
         )
@@ -385,10 +423,9 @@
 
     @pl.loop(0, groups)
     def _(g):
-        block = state[:, inside(g)]
-        pulled = over(dot16(mix[3], block)) * field[0, :, lanes(g)][None]
-        pulled = pulled + over(dot16(mix[4], block)) * field[1, :, lanes(g)][None]
-        pulled = pulled + over(dot16(mix[5], block)) * field[2, :, lanes(g)][None]
+        pulled = over(pulls[0, :, lanes(g)]) * field[0, :, lanes(g)][None]
+        pulled = pulled + over(pulls[1, :, lanes(g)]) * field[1, :, lanes(g)][None]
+        pulled = pulled + over(pulls[2, :, lanes(g)]) * field[2, :, lanes(g)][None]
         total[:, lanes(g)] = (
             total[:, lanes(g)]
             + pull * pulled.reshape(padded, GROUP)
@@ -413,7 +450,8 @@
         spots = jnp.broadcast_to(
             contact8[:, lanes(g)][None], (padded // 8, 8, GROUP)
         ).reshape(padded, GROUP)
-        out[:, lanes(g)] = (value * (plain + held * spots)).astype(jnp.bfloat16)
+        value = (value * (plain + held * spots))[0:count]
+        out[:, :, lanes(g)] = value.reshape(count // rows, rows, GROUP).astype(jnp.bfloat16)
 
     @pl.loop(0, groups)
     def _(g):
@@ -463,21 +501,6 @@
     names = tuple(constants)
     piece = round_up(Y // energy * rows, 8)
     groups = cells // GROUP
-    state = jnp.pad(
-        distribution.reshape(count, cells), ((0, padded - count), (LANE, LANE))
-    )
-    shape = (levels, harmonics, rows)
-    coef = jnp.stack(
-        [jnp.broadcast_to(level_coef[:, i][:, None, None], shape) for i in range(3)]
-        + [jnp.broadcast_to(phonon_kernel[i][:, :, None], shape) for i in range(2)]
-        + [jnp.broadcast_to(out_rate[:, :, None], shape)],
-        axis=-1,
-    ).reshape(count, 6)
-    coef = jnp.pad(coef, ((0, padded - count), (0, 2)))
-    wide = jnp.pad(
-        coupling.reshape(6, harmonics, harmonics).astype(jnp.float32),
-        ((0, 0), (0, LANE - harmonics), (0, LANE - harmonics)),
-    )
     vmem = pl.BlockSpec(memory_space=pltpu.VMEM)
     smem = pl.BlockSpec(memory_space=pltpu.SMEM)
     bf16, f32 = jnp.bfloat16, jnp.float32
@@ -487,12 +510,13 @@
             kernel, names, energy, space, rows, 1.0 / math.sqrt(levels * energy)
         ),
         out_shape=(
-            jax.ShapeDtypeStruct((padded, cells), bf16),
+            jax.ShapeDtypeStruct((levels * harmonics, rows, cells), bf16),
             jax.ShapeDtypeStruct((rows, cells), f32),
         ),
-        in_specs=[vmem] * (len(names) + 3) + [smem] + [vmem] * 2,
+        in_specs=[vmem] * (len(names) + 3) + [smem] + [vmem] * 5,
         out_specs=(vmem, vmem),
         scratch_shapes=[
+            pltpu.VMEM((padded, cells + 2 * LANE), bf16),
             pltpu.VMEM((padded, cells), bf16),
             pltpu.VMEM((padded, cells), bf16),
             pltpu.VMEM((2 * edge, cells), bf16),
@@ -500,14 +524,15 @@
             pltpu.VMEM((6, padded, padded), bf16),
             pltpu.VMEM((padded, 2 * edge), bf16),
             pltpu.VMEM((padded, cells), f32),
+            pltpu.VMEM((3, padded, cells), f32),
             pltpu.VMEM((8, cells), f32),
             pltpu.VMEM((groups * 8, GROUP), f32),
             pltpu.VMEM((energy, piece, LANE), f32),
             pltpu.VMEM((energy, piece, LANE), f32),
             pltpu.VMEM((piece, LANE), f32),
             pltpu.VMEM((space, piece, LANE), f32),
-            pltpu.VMEM((2 * piece, LANE), f32),
-            pltpu.VMEM((energy, 2 * piece, LANE), f32),
+            pltpu.VMEM((piece, LANE), f32),
+            pltpu.VMEM((energy, piece, LANE), f32),
             pltpu.VMEM((3, 8, cells), f32),
             pltpu.VMEM((8, cells), f32),
             dma((2, groups)),
@@ -531,14 +556,17 @@
         ),
     )(
         *[jnp.asarray(constants[name]) for name in names],
-        state,
+        distribution.reshape(levels * harmonics, rows, cells),
         region_map,
         contact_mask,
         doping_levels,
-        wide,
-        coef,
+        coupling,
+        level_coef,
+        level_coef.T,
+        phonon_kernel,
+        out_rate,
     )
-    return out[:count].reshape(distribution.shape), potential
+    return out.reshape(distribution.shape), potential
 
 
 def solution(mesh):

time: 69.3 us -> 69.3 us (level)
  local copies, waits for them, and re-layouts: 11.1 us -> 26.8 us
  Pallas kernels: 55.9 us -> 40.6 us
    unnamed x48 -> x59, local copies, waits for them, and re-layouts: 2.25 us -> 26.8 us
    pallas_call x1, Pallas kernels: 55.9 us -> 40.6 us  [local(): pl.pallas_call(functools.partial(kernel, names, energy, space, rows, 1.0...]
    reshape x2 -> x0, local copies, waits for them, and re-layouts: 4.21 us -> none  [the longest x1 2.67 us: local(): distribution.reshape(count, cells)]
    another operation x9 -> x0, local copies, waits for them, and re-layouts: 2.57 us -> none  [the longest x8 2.57 us: local(): jnp.stack([jnp.broadcast_to(level_coef[:, i][:, None, None], shape) for i...]
    pad x2 -> x0, local copies, waits for them, and re-layouts: 1.26 us -> none  [the longest x1 1.25 us: local(): jnp.pad(distribution.reshape(count, cells), ((0, padded - count), (LANE,...]
    slice x2 -> x0, local copies, waits for them, and re-layouts: 0.86 us -> none  [the longest x1 0.77 us: local(): phonon_kernel[i][:, :, None]]
where the time goes in v2:
time: 69.3 us; the launch traced here: 68 us
  Pallas kernels  40.6 us (59%)
  local copies, waits for them, and re-layouts  26.8 us (39%)
    pallas_call x1, Pallas kernels, local(): pl.pallas_call(functools.partial(kernel, names, energy, space, rows, 1.0...  40.6 us
    unnamed x59, local copies, waits for them, and re-layouts  26.8 us

profile of v2, /device:TPU:4, one launch (start us, length us, event | category | flops | bytes accessed | tf_op | source)
XLA Modules:
  0.0 68.0 jit_solution(610096646354884688)
XLA Ops:
  0.6 0.8 %copy.32.refs_26_ = f32[6,3]{1,0:T(8,128)S(1)} copy(f32[6,3]{0,1:T(4,128)} %param.34) | data formatting | bytes 144 | tf_op args[5]
  1.4 0.7 %copy.33.refs_28_ = f32[2,6,9]{2,1,0:T(8,128)S(1)} copy(f32[2,6,9]{2,0,1:T(2,128)} %param.35) | data formatting | bytes 864 | tf_op args[6]
  2.1 0.7 %copy.31.refs_25_ = bf16[2,3,9,9]{3,2,1,0:T(8,128)(2,1)S(1)} copy(bf16[2,3,9,9]{3,0,2,1:T(2,128)(2,1)} %param.33) | data formatting | bytes 1944 | tf_op args[4]
  2.8 0.0 copy-start
  2.8 0.7 copy-done
  3.5 0.0 copy-start.1
  3.5 1.3 %copy-done.1 = bf16[6,9,4,3072]{3,2,1,0:T(4,128)(2,1)S(1)} copy-done((bf16[6,9,4,3072]{3,2,1,0:T(4,128)(2,1)S(1)}, bf16[6,9,4,3072]{3,2,1,0:T(4,128)(2,1)}, u32[]{:S(2)}) %copy-start.1) | copy-done | bytes 1327128
  4.8 0.0 copy-start.2
  4.8 0.8 %copy-done.2 = s32[4,3072]{1,0:T(4,128)S(1)} copy-done((s32[4,3072]{1,0:T(4,128)S(1)}, s32[4,3072]{1,0:T(4,128)}, u32[]{:S(2)}) %copy-start.2) | copy-done | bytes 49176
  5.6 0.0 copy-start.3
  5.6 0.8 %copy-done.3 = s32[4,3072]{1,0:T(4,128)S(1)} copy-done((s32[4,3072]{1,0:T(4,128)S(1)}, s32[4,3072]{1,0:T(4,128)}, u32[]{:S(2)}) %copy-start.3) | copy-done | bytes 49176
  6.4 0.0 copy-start.4
  6.4 0.7 %copy-done.4 = f32[6,9]{1,0:T(8,128)S(1)} copy-done((f32[6,9]{1,0:T(8,128)S(1)}, f32[6,9]{1,0:T(8,128)}, u32[]{:S(2)}) %copy-start.4) | copy-done | bytes 240
  7.1 0.0 copy-start.5
  7.1 0.7 copy-done.5
  7.8 0.0 copy-start.6
  7.8 1.0 %copy-done.6 = f32[2,128,384]{2,1,0:T(8,128)S(1)} copy-done((f32[2,128,384]{2,1,0:T(8,128)S(1)}, f32[2,128,384]{2,1,0:T(8,128)}, u32[]{:S(2)}) %copy-start.6) | copy-done | bytes 393240
  8.8 0.0 copy-start.7
  8.8 1.0 %copy-done.7 = f32[256,384]{1,0:T(8,128)S(1)} copy-done((f32[256,384]{1,0:T(8,128)S(1)}, f32[256,384]{1,0:T(8,128)}, u32[]{:S(2)}) %copy-start.7) | copy-done | bytes 393240
  9.7 0.0 copy-start.8
  9.7 1.0 %copy-done.8 = f32[256,384]{1,0:T(8,128)S(1)} copy-done((f32[256,384]{1,0:T(8,128)S(1)}, f32[256,384]{1,0:T(8,128)}, u32[]{:S(2)}) %copy-start.8) | copy-done | bytes 393240
  10.7 0.0 copy-start.9
  10.7 1.0 %copy-done.9 = bf16[3,224,224]{2,1,0:T(8,128)(2,1)S(1)} copy-done((bf16[3,224,224]{2,1,0:T(8,128)(2,1)S(1)}, bf16[3,224,224]{2,1,0:T(8,128)(2,1)}, u32[]{:S(2)}) %copy-start.9) | copy-done | bytes 301080
  11.7 0.0 copy-start.10
  11.7 0.9 %copy-done.10 = f32[16,32,128]{2,1,0:T(8,128)S(1)} copy-done((f32[16,32,128]{2,1,0:T(8,128)S(1)}, f32[16,32,128]{2,1,0:T(8,128)}, u32[]{:S(2)}) %copy-start.10) | copy-done | bytes 262168
  12.7 0.0 copy-start.11
  12.7 0.9 %copy-done.11 = f32[2,8,3072]{2,1,0:T(8,128)S(1)} copy-done((f32[2,8,3072]{2,1,0:T(8,128)S(1)}, f32[2,8,3072]{2,1,0:T(8,128)}, u32[]{:S(2)}) %copy-start.11) | copy-done | bytes 196632
  13.6 0.0 copy-start.12
  13.6 0.9 %copy-done.12 = f32[384,128]{1,0:T(8,128)S(1)} copy-done((f32[384,128]{1,0:T(8,128)S(1)}, f32[384,128]{1,0:T(8,128)}, u32[]{:S(2)}) %copy-start.12) | copy-done | bytes 196632
  14.5 0.0 copy-start.13
  14.5 0.9 %copy-done.13 = f32[256,64]{1,0:T(8,128)S(1)} copy-done((f32[256,64]{1,0:T(8,128)S(1)}, f32[256,64]{1,0:T(8,128)}, u32[]{:S(2)}) %copy-start.13) | copy-done | bytes 65560
  15.4 0.0 copy-start.14
  15.4 0.9 %copy-done.14 = f32[256,64]{1,0:T(8,128)S(1)} copy-done((f32[256,64]{1,0:T(8,128)S(1)}, f32[256,64]{1,0:T(8,128)}, u32[]{:S(2)}) %copy-start.14) | copy-done | bytes 65560
  16.3 0.9 %copy-done.15 = f32[224,6]{1,0:T(8,128)S(1)} copy-done((f32[224,6]{1,0:T(8,128)S(1)}, f32[224,6]{1,0:T(8,128)}, u32[]{:S(2)}) %copy-start.15) | copy-done | bytes 5400
  17.2 0.9 %copy-done.16 = f32[224,9]{1,0:T(8,128)S(1)} copy-done((f32[224,9]{1,0:T(8,128)S(1)}, f32[224,9]{1,0:T(8,128)}, u32[]{:S(2)}) %copy-start.16) | copy-done | bytes 8088
  18.1 0.8 %copy-done.17 = f32[64,256]{1,0:T(8,128)S(1)} copy-done((f32[64,256]{1,0:T(8,128)S(1)}, f32[64,256]{1,0:T(8,128)}, u32[]{:S(2)}) %copy-start.17) | copy-done | bytes 65560
  19.0 0.8 %copy-done.18 = f32[64,256]{1,0:T(8,128)S(1)} copy-done((f32[64,256]{1,0:T(8,128)S(1)}, f32[64,256]{1,0:T(8,128)}, u32[]{:S(2)}) %copy-start.18) | copy-done | bytes 65560
  19.8 0.8 %copy-done.19 = bf16[128,224]{1,0:T(8,128)(2,1)S(1)} copy-done((bf16[128,224]{1,0:T(8,128)(2,1)S(1)}, bf16[128,224]{1,0:T(8,128)(2,1)}, u32[]{:S(2)}) %copy-start.19) | copy-done | bytes 57368
  20.7 0.8 %copy-done.20 = bf16[224,128]{1,0:T(8,128)(2,1)S(1)} copy-done((bf16[224,128]{1,0:T(8,128)(2,1)S(1)}, bf16[224,128]{1,0:T(8,128)(2,1)}, u32[]{:S(2)}) %copy-start.20) | copy-done | bytes 57368
  21.5 0.8 %copy-done.21 = f32[2,32,32]{2,1,0:T(8,128)S(1)} copy-done((f32[2,32,32]{2,1,0:T(8,128)S(1)}, f32[2,32,32]{2,1,0:T(8,128)}, u32[]{:S(2)}) %copy-start.21) | copy-done | bytes 8216
  22.2 0.7 %copy-done.22 = f32[32,32]{1,0:T(8,128)S(1)} copy-done((f32[32,32]{1,0:T(8,128)S(1)}, f32[32,32]{1,0:T(8,128)}, u32[]{:S(2)}) %copy-start.22) | copy-done | bytes 4120
  23.0 0.7 %copy-done.23 = f32[9,224]{1,0:T(8,128)S(1)} copy-done((f32[9,224]{1,0:T(8,128)S(1)}, f32[9,224]{1,0:T(8,128)}, u32[]{:S(2)}) %copy-start.23) | copy-done | bytes 8088
  23.7 0.7 %copy-done.24 = f32[6,224]{1,0:T(8,128)S(1)} copy-done((f32[6,224]{1,0:T(8,128)S(1)}, f32[6,224]{1,0:T(8,128)}, u32[]{:S(2)}) %copy-start.24) | copy-done | bytes 5400
  24.4 0.7 %copy-done.25 = f32[8,224]{1,0:T(8,128)S(1)} copy-done((f32[8,224]{1,0:T(8,128)S(1)}, f32[8,224]{1,0:T(8,128)}, u32[]{:S(2)}) %copy-start.25) | copy-done | bytes 7192
  25.1 0.7 %copy-done.26 = f32[9,128]{1,0:T(8,128)S(1)} copy-done((f32[9,128]{1,0:T(8,128)S(1)}, f32[9,128]{1,0:T(8,128)}, u32[]{:S(2)}) %copy-start.26) | copy-done | bytes 4632
  25.8 40.6 %shard_map.284 = (bf16[54,4,3072]{2,1,0:T(4,128)(2,1)S(1)}, f32[4,3072]{1,0:T(4,128)S(1)}) custom-call(f32[224,9]{1,0:T(8,128)S(1)} %copy-done.16, f32[9,224]{1,0:T(8,128)S(1)} %copy-done.23, f32[9,128]{1,0:T(8,128)S(1)} %copy-done.26, bf16[3,224,224]{2,1,0:T(8,128)(2,1)S(1)} %copy-done.9, bf16[224,128]{1,0:T(8,128)(2,1)S(1)} %copy-done.20, ...), custom_call_target="tpu_custom_call" | custom-call | flops 2157969408 | bytes 5505024 | tf_op jit(solution)/shard_map/pallas_call | solution.py:508
  66.3 1.1 %copy.36 = bf16[6,9,4,3072]{3,2,1,0:T(4,128)(2,1)} copy(bf16[6,9,4,3072]{3,2,1,0:T(4,128)(2,1)S(1)} %bitcast.3) | data formatting | bytes 2654208
  67.4 0.6 copy.37
  (12 shorter events, 0.0 us)
Async XLA Ops:
  2.8 0.7 %copy-start = (f32[6,3]{0,1:T(4,128)S(1)}, f32[6,3]{0,1:T(4,128)}, u32[]{:S(2)}) copy-start(f32[6,3]{0,1:T(4,128)} %param.34) | copy-start | bytes 220
  3.5 1.3 %copy-start.1 = (bf16[6,9,4,3072]{3,2,1,0:T(4,128)(2,1)S(1)}, bf16[6,9,4,3072]{3,2,1,0:T(4,128)(2,1)}, u32[]{:S(2)}) copy-start(bf16[6,9,4,3072]{3,2,1,0:T(4,128)(2,1)} %param.29) | copy-start | bytes 3981316
  4.8 0.8 %copy-start.2 = (s32[4,3072]{1,0:T(4,128)S(1)}, s32[4,3072]{1,0:T(4,128)}, u32[]{:S(2)}) copy-start(s32[4,3072]{1,0:T(4,128)} %refs_22_.1) | copy-start | bytes 147460
  5.6 0.8 %copy-start.3 = (s32[4,3072]{1,0:T(4,128)S(1)}, s32[4,3072]{1,0:T(4,128)}, u32[]{:S(2)}) copy-start(s32[4,3072]{1,0:T(4,128)} %refs_23_.1) | copy-start | bytes 147460
  6.4 0.7 %copy-start.4 = (f32[6,9]{1,0:T(8,128)S(1)}, f32[6,9]{1,0:T(8,128)}, u32[]{:S(2)}) copy-start(f32[6,9]{1,0:T(8,128)} %refs_29_.1) | copy-start | bytes 652
  7.1 0.7 copy-start.5
  7.8 1.0 %copy-start.6 = (f32[2,128,384]{2,1,0:T(8,128)S(1)}, f32[2,128,384]{2,1,0:T(8,128)}, u32[]{:S(2)}) copy-start(f32[2,128,384]{2,1,0:T(8,128)} %constant.58.clone.refs_16_) | copy-start | bytes 1179652
  8.8 1.0 %copy-start.7 = (f32[256,384]{1,0:T(8,128)S(1)}, f32[256,384]{1,0:T(8,128)}, u32[]{:S(2)}) copy-start(f32[256,384]{1,0:T(8,128)} %constant.56.clone.refs_14_) | copy-start | bytes 1179652
  9.7 1.0 %copy-start.8 = (f32[256,384]{1,0:T(8,128)S(1)}, f32[256,384]{1,0:T(8,128)}, u32[]{:S(2)}) copy-start(f32[256,384]{1,0:T(8,128)} %constant.55.clone.refs_13_) | copy-start | bytes 1179652
  10.7 1.0 %copy-start.9 = (bf16[3,224,224]{2,1,0:T(8,128)(2,1)S(1)}, bf16[3,224,224]{2,1,0:T(8,128)(2,1)}, u32[]{:S(2)}) copy-start(bf16[3,224,224]{2,1,0:T(8,128)(2,1)} %constant.45.clone.refs_3_) | copy-start | bytes 903172
  11.7 0.9 %copy-start.10 = (f32[16,32,128]{2,1,0:T(8,128)S(1)}, f32[16,32,128]{2,1,0:T(8,128)}, u32[]{:S(2)}) copy-start(f32[16,32,128]{2,1,0:T(8,128)} %constant.61.clone.refs_19_) | copy-start | bytes 786436
  12.7 0.9 %copy-start.11 = (f32[2,8,3072]{2,1,0:T(8,128)S(1)}, f32[2,8,3072]{2,1,0:T(8,128)}, u32[]{:S(2)}) copy-start(f32[2,8,3072]{2,1,0:T(8,128)} %constant.62.clone.refs_20_) | copy-start | bytes 589828
  13.6 0.9 %copy-start.12 = (f32[384,128]{1,0:T(8,128)S(1)}, f32[384,128]{1,0:T(8,128)}, u32[]{:S(2)}) copy-start(f32[384,128]{1,0:T(8,128)} %constant.57.clone.refs_15_) | copy-start | bytes 589828
  14.5 0.9 %copy-start.13 = (f32[256,64]{1,0:T(8,128)S(1)}, f32[256,64]{1,0:T(8,128)}, u32[]{:S(2)}) copy-start(f32[256,64]{1,0:T(8,128)} %constant.52.clone.refs_10_) | copy-start | bytes 196612
  15.4 0.9 %copy-start.14 = (f32[256,64]{1,0:T(8,128)S(1)}, f32[256,64]{1,0:T(8,128)}, u32[]{:S(2)}) copy-start(f32[256,64]{1,0:T(8,128)} %constant.51.clone.refs_9_) | copy-start | bytes 196612
  16.3 0.9 %copy-start.15 = (f32[224,6]{1,0:T(8,128)S(1)}, f32[224,6]{1,0:T(8,128)}, u32[]{:S(2)}) copy-start(f32[224,6]{1,0:T(8,128)} %constant.49.clone.refs_7_) | copy-start | bytes 16132
  17.2 0.9 %copy-start.16 = (f32[224,9]{1,0:T(8,128)S(1)}, f32[224,9]{1,0:T(8,128)}, u32[]{:S(2)}) copy-start(f32[224,9]{1,0:T(8,128)} %constant.42.clone.refs_0_) | copy-start | bytes 24196
  18.1 0.8 %copy-start.17 = (f32[64,256]{1,0:T(8,128)S(1)}, f32[64,256]{1,0:T(8,128)}, u32[]{:S(2)}) copy-start(f32[64,256]{1,0:T(8,128)} %constant.54.clone.refs_12_) | copy-start | bytes 196612
  19.0 0.8 %copy-start.18 = (f32[64,256]{1,0:T(8,128)S(1)}, f32[64,256]{1,0:T(8,128)}, u32[]{:S(2)}) copy-start(f32[64,256]{1,0:T(8,128)} %constant.53.clone.refs_11_) | copy-start | bytes 196612
  19.8 0.8 %copy-start.19 = (bf16[128,224]{1,0:T(8,128)(2,1)S(1)}, bf16[128,224]{1,0:T(8,128)(2,1)}, u32[]{:S(2)}) copy-start(bf16[128,224]{1,0:T(8,128)(2,1)} %constant.47.clone.refs_5_) | copy-start | bytes 172036
  20.7 0.8 %copy-start.20 = (bf16[224,128]{1,0:T(8,128)(2,1)S(1)}, bf16[224,128]{1,0:T(8,128)(2,1)}, u32[]{:S(2)}) copy-start(bf16[224,128]{1,0:T(8,128)(2,1)} %constant.46.clone.refs_4_) | copy-start | bytes 172036
  21.5 0.8 %copy-start.21 = (f32[2,32,32]{2,1,0:T(8,128)S(1)}, f32[2,32,32]{2,1,0:T(8,128)}, u32[]{:S(2)}) copy-start(f32[2,32,32]{2,1,0:T(8,128)} %constant.60.clone.refs_18_) | copy-start | bytes 24580
  22.2 0.7 %copy-start.22 = (f32[32,32]{1,0:T(8,128)S(1)}, f32[32,32]{1,0:T(8,128)}, u32[]{:S(2)}) copy-start(f32[32,32]{1,0:T(8,128)} %constant.59.clone.refs_17_) | copy-start | bytes 12292
  22.9 0.7 %copy-start.23 = (f32[9,224]{1,0:T(8,128)S(1)}, f32[9,224]{1,0:T(8,128)}, u32[]{:S(2)}) copy-start(f32[9,224]{1,0:T(8,128)} %constant.43.clone.refs_1_) | copy-start | bytes 24196
  23.7 0.7 %copy-start.24 = (f32[6,224]{1,0:T(8,128)S(1)}, f32[6,224]{1,0:T(8,128)}, u32[]{:S(2)}) copy-start(f32[6,224]{1,0:T(8,128)} %constant.50.clone.refs_8_) | copy-start | bytes 16132
  24.4 0.7 %copy-start.25 = (f32[8,224]{1,0:T(8,128)S(1)}, f32[8,224]{1,0:T(8,128)}, u32[]{:S(2)}) copy-start(f32[8,224]{1,0:T(8,128)} %constant.48.clone.refs_6_) | copy-start | bytes 21508
  25.1 0.7 %copy-start.26 = (f32[9,128]{1,0:T(8,128)S(1)}, f32[9,128]{1,0:T(8,128)}, u32[]{:S(2)}) copy-start(f32[9,128]{1,0:T(8,128)} %constant.44.clone.refs_2_) | copy-start | bytes 13828

commit v3 on v2

--- a/solution.py
+++ b/solution.py
@@ -128,8 +128,6 @@
         sin_in=sin_in, fold=fold, unfold=unfold, into=into, back=back, lam=lam, zmask=zmask,
     )
     values = {name: np.ascontiguousarray(value, f32) for name, value in values.items()}
-    for name in ("choose", "masks", "mask_edge"):
-        values[name] = values[name].astype(jnp.bfloat16)
     return values
 
 
@@ -137,19 +135,31 @@
     return jnp.dot(a, b, precision=highest, preferred_element_type=jnp.float32)
 
 
+def split(a):
+    high = a.astype(jnp.bfloat16)
+    return high, (a - high.astype(jnp.float32)).astype(jnp.bfloat16)
+
+
+def dot3(a, b):
+    (ah, al), (bh, bl) = split(a), split(b)
+    return dot16(ah, bh) + (dot16(ah, bl) + dot16(al, bh))
+
+
 def dot16(a, b):
     return jnp.dot(a, b, preferred_element_type=jnp.float32)
 
 
 def kernel(names, energy, space, rows, scale, *refs):
-    c = dict(zip(names, refs))
-    (given, region, contact, doping, coupling, level_coef, level_coef_t, phonon, out_rate) = refs[
-        len(names) : len(names) + 9
+    inputs = len(names) + 8
+    held_in = refs[inputs + 2 : 2 * inputs + 2]
+    c = dict(zip(names, held_in))
+    (given, region, contact, doping, coupling, level_coef_t, phonon, out_rate) = held_in[
+        len(names) :
     ]
-    out, potential = refs[len(names) + 9 : len(names) + 11]
+    out, potential = refs[inputs : inputs + 2]
     (state, above, below, edge_out, edge_in, mix, mix_edge, total, pulls, charge, folded, modes, got1, part,
-     got2, answer, got3, field, contact8, ssem, rsem, esend, erecv, s1, r1, s2, r2, s3, r3) = refs[
-        len(names) + 11 :
+     got2, answer, got3, field, contact8, isem, ssem, rsem, esend, erecv, s1, r1, s2, r2, s3, r3) = refs[
+        2 * inputs + 2 :
     ]
     padded, cells = above.shape
     edge = edge_in.shape[0] // 2
@@ -172,7 +182,12 @@
             barrier, inc=1, device_id={"space": lax.rem(slab + o, space)}, device_id_type=MESH
         )
 
-    pl.semaphore_wait(barrier, energy + space - 2)
+    def load(i):
+        return pltpu.make_async_copy(refs[i], held_in[i], isem.at[i])
+
+    order = [len(names)] + [i for i in range(inputs) if i != len(names)]
+    for i in order:
+        load(i).start()
 
     def lanes(g):
         return pl.ds(pl.multiple_of(g * GROUP, LANE), GROUP)
@@ -205,6 +220,7 @@
     state[:, 0:LANE] = jnp.zeros((padded, LANE), jnp.bfloat16)
     state[:, cells + LANE :] = jnp.zeros((padded, LANE), jnp.bfloat16)
     count = given.shape[0] * rows
+    load(order[0]).wait()
 
     @pl.loop(0, groups)
     def _(g):
@@ -213,7 +229,10 @@
         state[:, inside(g)] = block.astype(jnp.bfloat16)
 
     first, second, third = groups // 4, groups // 2, groups * 5 // 8
+    pl.semaphore_wait(barrier, energy + space - 2)
     send_levels(0, first)
+    for i in order[1:]:
+        load(i).wait()
 
     density = dot32(level_coef_t[...], c["pick_level_t"][...])[2:3, :]
     weight = c["dense"][...] * density * scale
@@ -221,25 +240,21 @@
     rest = weight - high.astype(jnp.float32)
     middle = rest.astype(jnp.bfloat16)
     low = (rest - middle.astype(jnp.float32)).astype(jnp.bfloat16)
-    weights = jnp.concatenate([high, middle], axis=0)
-    weights_low = jnp.concatenate([low, jnp.zeros_like(low)], axis=0)
+    weights = jnp.concatenate([high, middle, low, jnp.zeros_like(low)], axis=0)
     mine = jnp.where(me == 0, 1.0, 0.0).astype(jnp.float32)
 
     charge[...] = jnp.zeros_like(charge)
     for row in range(0, 8, rows):
         contact8[row : row + rows, :] = contact[...].astype(jnp.float32)
     found = jnp.zeros(region.shape, jnp.float32)
-    for kind in range(doping.shape[0]):
-        found = found + jnp.where(region[...] == kind, doping[kind], 0.0)
+    for kind in range(doping.shape[1]):
+        found = found + jnp.where(region[...] == kind, doping[0:1, kind : kind + 1], 0.0)
     charge[0:rows, :] = -found * mine
-    choose = c["choose"][...]
     for g in range(groups):
         span = slice(g * GROUP, (g + 1) * GROUP)
         block = state[:, g * GROUP + LANE : (g + 1) * GROUP + LANE]
         parts = dot16(weights, block)
-        fine = dot16(weights_low, block)
-        folded[g * 8 : (g + 1) * 8, :] = parts[0:8] + (parts[8:16] + fine[0:8]) + charge[:, span]
-        edge_out[:, span] = dot16(choose, block).astype(jnp.bfloat16)
+        folded[g * 8 : (g + 1) * 8, :] = parts[0:8] + (parts[8:16] + parts[16:24]) + charge[:, span]
 
     def edge_copy(up):
         target = jnp.minimum(slab + 1, space - 1) if up else jnp.maximum(slab - 1, 0)
@@ -255,10 +270,10 @@
         )
 
     charges = folded[...]
-    turned = c["sin_in"][...] * dot32(c["fc"][...], charges) + c["cos_in"][...] * dot32(
+    turned = c["sin_in"][...] * dot3(c["fc"][...], charges) + c["cos_in"][...] * dot3(
         c["fs"][...], charges
     )
-    modes[...] = dot32(turned, c["fold"][...]).reshape(modes.shape)
+    modes[...] = dot3(turned, c["fold"][...]).reshape(modes.shape)
 
     def spread(source, fixed, got, sends, recvs, o, sending):
         other = lax.rem(me + o, energy) if sending else lax.rem(me + energy - o, energy)
@@ -277,11 +292,18 @@
 
     send_levels(first, second)
 
+    choose = c["choose"][...].astype(jnp.bfloat16)
+
+    @pl.loop(0, groups)
+    def _(g):
+        edge_out[:, lanes(g)] = dot16(choose, state[:, inside(g)]).astype(jnp.bfloat16)
+
     pick, pick_t = c["pick"][...], c["pick_t"][...]
+    slots = (0, 5, 1, 2, 3, 4)
     for d in range(6):
-        wide = dot16(pick, coupling[d // 3, d % 3].astype(jnp.float32))
-        mask = c["masks"][0 if d == 0 else 1 if d < 3 else 2].astype(jnp.float32)
-        mix[d] = (dot16(wide, pick_t) * mask).astype(jnp.bfloat16)
+        wide = dot16(pick, coupling[d % 3].astype(jnp.float32)[:, d // 3, :])
+        mask = c["masks"][0 if d == 0 else 1 if d < 3 else 2]
+        mix[slots[d] * padded : (slots[d] + 1) * padded, :] = (dot16(wide, pick_t) * mask).astype(jnp.bfloat16)
         if d == 0:
             mix_edge[...] = (dot16(wide, c["pick_edge"][...]) * c["mask_edge"][...]).astype(
                 jnp.bfloat16
@@ -290,29 +312,41 @@
     def by_row(values):
         return jnp.sum(dot32(c["pick_level"][...], values) * pick, axis=1, keepdims=True)
 
-    coef = dot32(c["pick_level"][...], level_coef[...])
+    coef = lax.dot_general(
+        c["pick_level"][...],
+        level_coef_t[...],
+        (((1,), (1,)), ((), ())),
+        precision=highest,
+        preferred_element_type=jnp.float32,
+    )
     speed = step_time * coef[:, 0:1]
     pull = (step_time * 3.0) * coef[:, 1:2]
-    rate_up = step_time * by_row(phonon[0])
-    rate_down = step_time * by_row(phonon[1])
+    rate_up = step_time * by_row(phonon[:, 0, :])
+    rate_down = step_time * by_row(phonon[:, 1, :])
     decay = by_row(out_rate[...])
     plain = 1.0 / (1.0 + step_time * decay)
     held = 1.0 / (1.0 + step_time * (decay + contact_rate)) - plain
 
-    @pl.loop(0, groups)
-    def _(g):
+    def mix_group(g):
         block = state[:, inside(g)]
-        around = state[:, pl.ds(pl.multiple_of(g * GROUP, LANE), GROUP + 2 * LANE)]
         size = GROUP + 2 * LANE
-        ty = dot16(mix[1], around)
+        around = state[:, pl.ds(pl.multiple_of(g * GROUP, LANE), size)]
+        ty = dot16(mix[5 * padded :], around)
         ty = (pltpu.roll(ty, size - Z, axis=1) - pltpu.roll(ty, Z, axis=1))[:, LANE : LANE + GROUP]
-        tz = dot16(mix[2], block)
+        mixed = dot16(mix[0 : 5 * padded], block)
+        tz = mixed[padded : 2 * padded]
         tz = pltpu.roll(tz, GROUP - 1, axis=1) * c["zmask"][1, 0:1, 0:GROUP] - pltpu.roll(
             tz, 1, axis=1
         ) * c["zmask"][0, 0:1, 0:GROUP]
-        total[:, lanes(g)] = block.astype(jnp.float32) - speed * (dot16(mix[0], block) + ty + tz)
+        total[:, lanes(g)] = block.astype(jnp.float32) - speed * (mixed[0:padded] + ty + tz)
         for d in range(3):
-            pulls[d, :, lanes(g)] = dot16(mix[3 + d], block)
+            pulls[d, :, lanes(g)] = mixed[(2 + d) * padded : (3 + d) * padded]
+
+    early = groups // 4
+
+    @pl.loop(0, early)
+    def _(g):
+        mix_group(g)
 
     @pl.loop(1, energy)
     def _(o):
@@ -367,13 +401,17 @@
     send_levels(third, groups)
     got3[me] = answer[...]
 
+    @pl.loop(early, groups)
+    def _(g):
+        mix_group(g)
+
     @pl.loop(1, energy)
     def _(o):
         spread(answer, True, got3, s3, r3, o, False).wait_recv()
 
     for which in range(2):
-        lines = dot32(got3[...].reshape(energy * piece, LANE), c["unfold"][which])
-        lines = dot32(c["bs"][...], c["cos_in"][...] * lines) + dot32(
+        lines = dot3(got3[...].reshape(energy * piece, LANE), c["unfold"][which])
+        lines = dot3(c["bs"][...], c["cos_in"][...] * lines) + dot3(
             c["bc"][...], c["sin_in"][...] * lines
         )
         for g in range(groups):
@@ -502,7 +540,16 @@
     piece = round_up(Y // energy * rows, 8)
     groups = cells // GROUP
     vmem = pl.BlockSpec(memory_space=pltpu.VMEM)
-    smem = pl.BlockSpec(memory_space=pltpu.SMEM)
+    operands = [jnp.asarray(constants[name]) for name in names] + [
+        distribution.reshape(levels * harmonics, rows, cells),
+        region_map,
+        contact_mask,
+        doping_levels.reshape(1, -1),
+        coupling.transpose(1, 2, 0, 3),
+        level_coef.T,
+        phonon_kernel.transpose(1, 0, 2),
+        out_rate,
+    ]
     bf16, f32 = jnp.bfloat16, jnp.float32
     dma = pltpu.SemaphoreType.DMA
     out, potential = pl.pallas_call(
@@ -513,15 +560,16 @@
             jax.ShapeDtypeStruct((levels * harmonics, rows, cells), bf16),
             jax.ShapeDtypeStruct((rows, cells), f32),
         ),
-        in_specs=[vmem] * (len(names) + 3) + [smem] + [vmem] * 5,
+        in_specs=[pl.BlockSpec(memory_space=pl.ANY)] * len(operands),
         out_specs=(vmem, vmem),
-        scratch_shapes=[
+        scratch_shapes=[pltpu.VMEM(value.shape, value.dtype) for value in operands]
+        + [
             pltpu.VMEM((padded, cells + 2 * LANE), bf16),
             pltpu.VMEM((padded, cells), bf16),
             pltpu.VMEM((padded, cells), bf16),
             pltpu.VMEM((2 * edge, cells), bf16),
             pltpu.VMEM((2 * edge, cells), bf16),
-            pltpu.VMEM((6, padded, padded), bf16),
+            pltpu.VMEM((6 * padded, padded), bf16),
             pltpu.VMEM((padded, 2 * edge), bf16),
             pltpu.VMEM((padded, cells), f32),
             pltpu.VMEM((3, padded, cells), f32),
@@ -535,6 +583,7 @@
             pltpu.VMEM((energy, piece, LANE), f32),
             pltpu.VMEM((3, 8, cells), f32),
             pltpu.VMEM((8, cells), f32),
+            dma((len(operands),)),
             dma((2, groups)),
             dma((2, groups)),
             dma((2,)),
@@ -547,25 +596,14 @@
             dma((energy,)),
         ],
         compiler_params=pltpu.CompilerParams(
-            collective_id=0, has_side_effects=True, vmem_limit_bytes=48 * 1024 * 1024
+            collective_id=0, has_side_effects=True, vmem_limit_bytes=56 * 1024 * 1024
         ),
         cost_estimate=pl.CostEstimate(
             flops=2 * 7 * padded * padded * cells,
             bytes_accessed=8 * padded * cells,
             transcendentals=0,
         ),
-    )(
-        *[jnp.asarray(constants[name]) for name in names],
-        distribution.reshape(levels * harmonics, rows, cells),
-        region_map,
-        contact_mask,
-        doping_levels,
-        coupling,
-        level_coef,
-        level_coef.T,
-        phonon_kernel,
-        out_rate,
-    )
+    )(*operands)
     return out.reshape(distribution.shape), potential
 
 

time: 69.3 us -> 45.4 us (0.66); the launches traced: 68 us -> 45.2 us
  local copies, waits for them, and re-layouts: 26.8 us -> 3.48 us
    unnamed x59 -> x4, local copies, waits for them, and re-layouts: 26.8 us -> 3.48 us
where the time goes in v3:
time: 45.4 us; the launch traced here: 45.2 us
  Pallas kernels  41.1 us (91%)
  local copies, waits for them, and re-layouts  3.48 us (8%)
  between operations  0.65 us (1%)
    pallas_call x1, Pallas kernels, local(): pl.pallas_call(functools.partial(kernel, names, energy, space, rows, 1.0...  41.1 us
    unnamed x4, local copies, waits for them, and re-layouts  3.48 us

profile of v3, /device:TPU:4, one launch (start us, length us, event | category | flops | bytes accessed | tf_op | source)
XLA Modules:
  0.0 45.2 jit_solution(6168437146062782279)
XLA Ops:
  0.6 41.1 %shard_map.284 = (bf16[54,4,3072]{2,1,0:T(4,128)(2,1)}, f32[4,3072]{1,0:T(4,128)}) custom-call(f32[224,9]{1,0:T(8,128)} %constant.42.clone.refs_0_, f32[9,224]{1,0:T(8,128)} %constant.43.clone.refs_1_, f32[9,128]{1,0:T(8,128)} %constant.44.clone.refs_2_, f32[3,224,224]{2,1,0:T(8,128)} %constant.45.clone.refs_3_, f32[224,128]{1,0:T(8,128)} %constant.46.clone.refs_4_, ...), custom_call_target="tpu_custom_call" | custom-call | flops 2157969408 | bytes 5505024 | tf_op jit(solution)/shard_map/pallas_call | solution.py:555
  41.8 0.0 copy-start
  41.8 2.9 %copy.33 = bf16[6,9,4,3072]{3,2,1,0:T(4,128)(2,1)} copy(bf16[6,9,4,3072]{3,2,1,0:T(4,128)(2,1)} %bitcast.6) | data formatting | bytes 2654208
  44.6 0.0 copy-done
  44.6 0.6 %copy.34 = f32[4,3072]{1,0:T(4,128)} copy(f32[4,3072]{1,0:T(4,128)S(1)} %copy-done) | data formatting | bytes 98304
Async XLA Ops:
  41.8 2.9 %copy-start = (f32[4,3072]{1,0:T(4,128)S(1)}, f32[4,3072]{1,0:T(4,128)}, u32[]{:S(2)}) copy-start(f32[4,3072]{1,0:T(4,128)} %get-tuple-element.9) | copy-start | bytes 147460

commit v4 on v3

--- a/solution.py
+++ b/solution.py
@@ -222,15 +222,24 @@
     count = given.shape[0] * rows
     load(order[0]).wait()
 
-    @pl.loop(0, groups)
-    def _(g):
+    def lay_out(g):
         block = given[:, :, lanes(g)].astype(jnp.float32).reshape(count, GROUP)
         block = jnp.concatenate([block, jnp.zeros((padded - count, GROUP), jnp.float32)], axis=0)
         state[:, inside(g)] = block.astype(jnp.bfloat16)
 
-    first, second, third = groups // 4, groups // 2, groups * 5 // 8
+    first, second, third = groups // 4, groups * 5 // 8, groups * 3 // 4
+
+    @pl.loop(0, first)
+    def _(g):
+        lay_out(g)
+
     pl.semaphore_wait(barrier, energy + space - 2)
     send_levels(0, first)
+
+    @pl.loop(first, groups)
+    def _(g):
+        lay_out(g)
+
     for i in order[1:]:
         load(i).wait()
 

time: 45.4 us -> 46.2 us (1.018)
  Pallas kernels: 41.1 us -> 41.7 us
    pallas_call x1, Pallas kernels: 41.1 us -> 41.7 us  [local(): pl.pallas_call(functools.partial(kernel, names, energy, space, rows, 1.0...]
where the time goes in v4:
time: 46.2 us; the launch traced here: 45.8 us
  Pallas kernels  41.7 us (90%)
  local copies, waits for them, and re-layouts  3.48 us (8%)
  between operations  0.65 us (1%)
    pallas_call x1, Pallas kernels, local(): pl.pallas_call(functools.partial(kernel, names, energy, space, rows, 1.0...  41.7 us
    unnamed x4, local copies, waits for them, and re-layouts  3.48 us

profile of v4, /device:TPU:4, one launch (start us, length us, event | category | flops | bytes accessed | tf_op | source)
XLA Modules:
  0.0 45.8 jit_solution(16897108244977376852)
XLA Ops:
  0.6 41.7 %shard_map.284 = (bf16[54,4,3072]{2,1,0:T(4,128)(2,1)}, f32[4,3072]{1,0:T(4,128)}) custom-call(f32[224,9]{1,0:T(8,128)} %constant.42.clone.refs_0_, f32[9,224]{1,0:T(8,128)} %constant.43.clone.refs_1_, f32[9,128]{1,0:T(8,128)} %constant.44.clone.refs_2_, f32[3,224,224]{2,1,0:T(8,128)} %constant.45.clone.refs_3_, f32[224,128]{1,0:T(8,128)} %constant.46.clone.refs_4_, ...), custom_call_target="tpu_custom_call" | custom-call | flops 2157969408 | bytes 5505024 | tf_op jit(solution)/shard_map/pallas_call | solution.py:564
  42.3 0.0 copy-start
  42.3 2.9 %copy.33 = bf16[6,9,4,3072]{3,2,1,0:T(4,128)(2,1)} copy(bf16[6,9,4,3072]{3,2,1,0:T(4,128)(2,1)} %bitcast.6) | data formatting | bytes 2654208
  45.2 0.0 copy-done
  45.2 0.6 %copy.34 = f32[4,3072]{1,0:T(4,128)} copy(f32[4,3072]{1,0:T(4,128)S(1)} %copy-done) | data formatting | bytes 98304
Async XLA Ops:
  42.3 2.9 %copy-start = (f32[4,3072]{1,0:T(4,128)S(1)}, f32[4,3072]{1,0:T(4,128)}, u32[]{:S(2)}) copy-start(f32[4,3072]{1,0:T(4,128)} %get-tuple-element.9) | copy-start | bytes 147460

commit v5 on v4

--- a/solution.py
+++ b/solution.py
@@ -227,7 +227,7 @@
         block = jnp.concatenate([block, jnp.zeros((padded - count, GROUP), jnp.float32)], axis=0)
         state[:, inside(g)] = block.astype(jnp.bfloat16)
 
-    first, second, third = groups // 4, groups * 5 // 8, groups * 3 // 4
+    first, second, third = groups // 4, groups * 3 // 8, groups // 2
 
     @pl.loop(0, first)
     def _(g):
@@ -413,6 +413,34 @@
     @pl.loop(early, groups)
     def _(g):
         mix_group(g)
+
+    @pl.when(slab > 0)
+    def _():
+        edge_copy(True).wait_recv()
+
+    @pl.when(slab == 0)
+    def _():
+        edge_in[0:edge, :] = jnp.zeros((edge, cells), jnp.bfloat16)
+
+    @pl.when(slab < space - 1)
+    def _():
+        edge_copy(False).wait_recv()
+
+    @pl.when(slab == space - 1)
+    def _():
+        edge_in[edge : 2 * edge, :] = jnp.zeros((edge, cells), jnp.bfloat16)
+
+    @pl.when(me == 0)
+    def _():
+        below[...] = jnp.zeros_like(below)
+
+    @pl.when(me == energy - 1)
+    def _():
+        above[...] = jnp.zeros_like(above)
+
+    @pl.loop(0, groups)
+    def _(g):
+        total[:, lanes(g)] -= speed * dot16(mix_edge[...], edge_in[:, lanes(g)])
 
     @pl.loop(1, energy)
     def _(o):
@@ -441,30 +469,6 @@
         - c["zmask"][1] * pltpu.roll(level, cells - 1, axis=1)
     )
 
-    @pl.when(slab > 0)
-    def _():
-        edge_copy(True).wait_recv()
-
-    @pl.when(slab == 0)
-    def _():
-        edge_in[0:edge, :] = jnp.zeros((edge, cells), jnp.bfloat16)
-
-    @pl.when(slab < space - 1)
-    def _():
-        edge_copy(False).wait_recv()
-
-    @pl.when(slab == space - 1)
-    def _():
-        edge_in[edge : 2 * edge, :] = jnp.zeros((edge, cells), jnp.bfloat16)
-
-    @pl.when(me == 0)
-    def _():
-        below[...] = jnp.zeros_like(below)
-
-    @pl.when(me == energy - 1)
-    def _():
-        above[...] = jnp.zeros_like(above)
-
     def over(values):
         return values.reshape(padded // 8, 8, GROUP)
 
@@ -473,14 +477,7 @@
         pulled = over(pulls[0, :, lanes(g)]) * field[0, :, lanes(g)][None]
         pulled = pulled + over(pulls[1, :, lanes(g)]) * field[1, :, lanes(g)][None]
         pulled = pulled + over(pulls[2, :, lanes(g)]) * field[2, :, lanes(g)][None]
-        total[:, lanes(g)] = (
-            total[:, lanes(g)]
-            + pull * pulled.reshape(padded, GROUP)
-            - speed * dot16(mix_edge[...], edge_in[:, lanes(g)])
-        )
-
-    @pl.loop(0, groups)
-    def _(g):
+
         @pl.when(me > 0)
         def _():
             level_copy(g, True).wait_recv()
@@ -491,6 +488,7 @@
 
         value = (
             total[:, lanes(g)]
+            + pull * pulled.reshape(padded, GROUP)
             + rate_up * above[:, lanes(g)].astype(jnp.float32)
             + rate_down * below[:, lanes(g)].astype(jnp.float32)
         )

time: 46.2 us -> 45.5 us (0.985)
  Pallas kernels: 41.7 us -> 41.2 us
    pallas_call x1, Pallas kernels: 41.7 us -> 41.2 us  [local(): pl.pallas_call(functools.partial(kernel, names, energy, space, rows, 1.0...]
where the time goes in v5:
time: 45.5 us; the launch traced here: 45.3 us
  Pallas kernels  41.2 us (91%)
  local copies, waits for them, and re-layouts  3.48 us (8%)
  between operations  0.65 us (1%)
    pallas_call x1, Pallas kernels, local(): pl.pallas_call(functools.partial(kernel, names, energy, space, rows, 1.0...  41.2 us
    unnamed x4, local copies, waits for them, and re-layouts  3.48 us

profile of v5, /device:TPU:4, one launch (start us, length us, event | category | flops | bytes accessed | tf_op | source)
XLA Modules:
  0.0 45.3 jit_solution(12756489447181014389)
XLA Ops:
  0.6 41.2 %shard_map.284 = (bf16[54,4,3072]{2,1,0:T(4,128)(2,1)}, f32[4,3072]{1,0:T(4,128)}) custom-call(f32[224,9]{1,0:T(8,128)} %constant.42.clone.refs_0_, f32[9,224]{1,0:T(8,128)} %constant.43.clone.refs_1_, f32[9,128]{1,0:T(8,128)} %constant.44.clone.refs_2_, f32[3,224,224]{2,1,0:T(8,128)} %constant.45.clone.refs_3_, f32[224,128]{1,0:T(8,128)} %constant.46.clone.refs_4_, ...), custom_call_target="tpu_custom_call" | custom-call | flops 2157969408 | bytes 5505024 | tf_op jit(solution)/shard_map/pallas_call | solution.py:562
  41.8 0.0 copy-start
  41.8 2.9 %copy.33 = bf16[6,9,4,3072]{3,2,1,0:T(4,128)(2,1)} copy(bf16[6,9,4,3072]{3,2,1,0:T(4,128)(2,1)} %bitcast.6) | data formatting | bytes 2654208
  44.7 0.0 copy-done
  44.7 0.6 %copy.34 = f32[4,3072]{1,0:T(4,128)} copy(f32[4,3072]{1,0:T(4,128)S(1)} %copy-done) | data formatting | bytes 98304
Async XLA Ops:
  41.8 2.9 %copy-start = (f32[4,3072]{1,0:T(4,128)S(1)}, f32[4,3072]{1,0:T(4,128)}, u32[]{:S(2)}) copy-start(f32[4,3072]{1,0:T(4,128)} %get-tuple-element.9) | copy-start | bytes 147460

commit v6 on v5

--- a/solution.py
+++ b/solution.py
@@ -206,14 +206,16 @@
             device_id_type=MESH,
         )
 
-    def send_levels(first, last):
+    odd = lax.rem(me, 2)
+
+    def send_levels(first, last, outward=True):
         @pl.loop(first, last)
         def _(g):
-            @pl.when(me < energy - 1)
+            @pl.when((me < energy - 1) & (odd == (1 if outward else 0)))
             def _():
                 level_copy(g, True).start()
 
-            @pl.when(me > 0)
+            @pl.when((me > 0) & (odd == (0 if outward else 1)))
             def _():
                 level_copy(g, False).start()
 
@@ -227,7 +229,7 @@
         block = jnp.concatenate([block, jnp.zeros((padded - count, GROUP), jnp.float32)], axis=0)
         state[:, inside(g)] = block.astype(jnp.bfloat16)
 
-    first, second, third = groups // 4, groups * 3 // 8, groups // 2
+    first, second, third = groups // 4, groups // 2, groups * 5 // 8
 
     @pl.loop(0, first)
     def _(g):
@@ -408,6 +410,7 @@
         spread(answer, True, got3, s3, r3, o, True).start()
 
     send_levels(third, groups)
+    send_levels(0, groups, False)
     got3[me] = answer[...]
 
     @pl.loop(early, groups)

time: 45.5 us -> 45.4 us (level)
  no operation moved by 1% of the time
where the time goes in v6:
time: 45.4 us; the launch traced here: 45.3 us
  Pallas kernels  41.2 us (91%)
  local copies, waits for them, and re-layouts  3.48 us (8%)
  between operations  0.65 us (1%)
    pallas_call x1, Pallas kernels, local(): pl.pallas_call(functools.partial(kernel, names, energy, space, rows, 1.0...  41.2 us
    unnamed x4, local copies, waits for them, and re-layouts  3.48 us

profile of v6, /device:TPU:4, one launch (start us, length us, event | category | flops | bytes accessed | tf_op | source)
XLA Modules:
  0.0 45.3 jit_solution(8069796047901425715)
XLA Ops:
  0.6 41.2 %shard_map.284 = (bf16[54,4,3072]{2,1,0:T(4,128)(2,1)}, f32[4,3072]{1,0:T(4,128)}) custom-call(f32[224,9]{1,0:T(8,128)} %constant.42.clone.refs_0_, f32[9,224]{1,0:T(8,128)} %constant.43.clone.refs_1_, f32[9,128]{1,0:T(8,128)} %constant.44.clone.refs_2_, f32[3,224,224]{2,1,0:T(8,128)} %constant.45.clone.refs_3_, f32[224,128]{1,0:T(8,128)} %constant.46.clone.refs_4_, ...), custom_call_target="tpu_custom_call" | custom-call | flops 2157969408 | bytes 5505024 | tf_op jit(solution)/shard_map/pallas_call | solution.py:565
  41.8 0.0 copy-start
  41.8 2.9 %copy.33 = bf16[6,9,4,3072]{3,2,1,0:T(4,128)(2,1)} copy(bf16[6,9,4,3072]{3,2,1,0:T(4,128)(2,1)} %bitcast.6) | data formatting | bytes 2654208
  44.7 0.0 copy-done
  44.7 0.6 %copy.34 = f32[4,3072]{1,0:T(4,128)} copy(f32[4,3072]{1,0:T(4,128)S(1)} %copy-done) | data formatting | bytes 98304
Async XLA Ops:
  41.8 2.9 %copy-start = (f32[4,3072]{1,0:T(4,128)S(1)}, f32[4,3072]{1,0:T(4,128)}, u32[]{:S(2)}) copy-start(f32[4,3072]{1,0:T(4,128)} %get-tuple-element.9) | copy-start | bytes 147460
